TPU v7x, 256 devices: a whole 4x4x8 slice. The times are simulated.
256 devices in a mesh: dp: 4 (over z_hi, core), grid: 64 (over x, z_lo, y).
Axes of the slice: x: 4, y: 4, z: 8 (z_hi: 2, z_lo: 4; z = z_hi * 4 + z_lo), core: 2. Of those that a mesh axis runs over, the one named last changes fastest.
Arguments:
- snapshots: bfloat16 [4, 64, 128, 64, 128], P('dp', None, 'grid'), may hold values from -6 to 6
- cotangent: bfloat16 [4, 32, 128, 64, 128], P('dp', None, 'grid'), may hold values from -6 to 6
- local_weight: bfloat16 [64, 32], replicated, may hold values from -0.75 to 0.75
- spectral_weight: float32 [32, 512, 4096], P('dp', 'grid'), may hold values from -6 to 6
- first_moment: float32 [32, 512, 4096], P('dp', 'grid'), may hold values from -6 to 6
- second_moment: float32 [32, 512, 4096], P('dp', 'grid'), may hold values from 1 to 30
Outputs:
- grad_input: bfloat16 [4, 64, 128, 64, 128], P('dp', None, 'grid')
- local_grad: float32 [64, 32], replicated
- new_weight: float32 [32, 512, 4096], P('dp', 'grid')
- new_first: float32 [32, 512, 4096], P('dp', 'grid')
- new_second: float32 [32, 512, 4096], P('dp', 'grid')
All inputs are finite; a program needn't handle non-finite values.
Results may differ from a plain program's by a relative error of at most 0.0056.
Values sent between devices are 32-bit elements; how exact they have to be, the bound alone decides.
A program may use at most 128 MiB of HBM per device.

v0:
```python
import math

import jax
import jax.numpy as jnp
from jax import lax
from jax.sharding import PartitionSpec as P

NX = 128
NY = 64
NZ = 128
KX = 32
KY = 32
KZ = 16
STEP = 100


highest = lax.Precision.HIGHEST
learning_rate = 0.02


def mode_numbers(length, retained):
    indices = jnp.arange(retained, dtype=jnp.int32)
    return jnp.where(indices < retained // 2, indices, length - retained + indices)


def phase_table(length, numbers):
    points = jnp.arange(length, dtype=jnp.int32)
    windings = points[:, None] * numbers[None, :] % length
    return windings.astype(jnp.float32) * (2.0 * math.pi / length)


def rotation(angles, direction, scaling):
    cosine = jnp.cos(angles) * scaling
    sine_part = direction * jnp.sin(angles) * scaling
    return jnp.stack([jnp.stack([cosine, sine_part]), jnp.stack([-sine_part, cosine])])


def forward_tables(z_scale):
    z_angles = phase_table(NZ, jnp.arange(KZ, dtype=jnp.int32))
    z_table = jnp.stack(
        [jnp.cos(z_angles) * z_scale[None, :], -jnp.sin(z_angles) * z_scale[None, :]], axis=1
    ).astype(jnp.bfloat16)
    y_table = rotation(phase_table(NY, mode_numbers(NY, KY)), -1.0, 1.0)
    x_table = rotation(phase_table(NX, mode_numbers(NX, KX)), -1.0, 1.0)
    return (z_table, y_table, x_table)


def inverse_tables(z_scale):
    x_table = rotation(phase_table(NX, mode_numbers(NX, KX)).T, 1.0, 1.0)
    y_table = rotation(phase_table(NY, mode_numbers(NY, KY)).T, 1.0, 1.0)
    z_angles = phase_table(NZ, jnp.arange(KZ, dtype=jnp.int32)).T
    z_table = jnp.stack(
        [z_scale[:, None] * jnp.cos(z_angles), -z_scale[:, None] * jnp.sin(z_angles)]
    )
    return (x_table, y_table, z_table)


def forward_modes(values, tables):
    z_table, y_table, x_table = tables
    partial_z = jnp.einsum("ncxyz,zrq->ncxyrq", values, z_table, preferred_element_type=jnp.float32)
    partial_y = jnp.einsum("ncxyrq,rsyk->nsxkqc", partial_z, y_table, precision=highest)
    snapshot_count = partial_y.shape[0]
    slab_width = partial_y.shape[2]
    channel_count = partial_y.shape[-1]
    flattened = partial_y.reshape(snapshot_count, 2, slab_width, KY * KZ * channel_count)
    received = lax.all_to_all(flattened, "grid", split_axis=3, concat_axis=2, tiled=True)
    item_count = received.shape[0]
    shaped = received.reshape(item_count, 2, NX, -1, channel_count)
    return jnp.einsum("nsxmc,stxk->ntkmc", shaped, x_table, precision=highest)


def inverse_modes(spectra, tables):
    x_table, y_table, z_table = tables
    along_x = jnp.einsum("nrkmo,rskx->nsxmo", spectra, x_table, precision=highest)
    snapshot_count = along_x.shape[0]
    owned_modes = along_x.shape[3]
    channel_count = along_x.shape[-1]
    flattened = along_x.reshape(snapshot_count, 2, NX, owned_modes * channel_count)
    block_in = lax.all_to_all(flattened, "grid", split_axis=2, concat_axis=3, tiled=True)
    item_count = block_in.shape[0]
    slab_width = block_in.shape[2]
    shaped = block_in.reshape(item_count, 2, slab_width, KY, KZ, channel_count)
    along_y = jnp.einsum("nrxkqo,rsky->noxysq", shaped, y_table, precision=highest)
    return jnp.einsum("noxysq,sqz->noxyz", along_y, z_table, precision=highest)


def mix_modes(spectra, weights):

    def product(left_part, right_part):
        return jnp.einsum("nkmi,kmio->nkmo", left_part, right_part, precision=highest)

    real_part = product(spectra[:, 0], weights[:, :, 0]) - product(spectra[:, 1], weights[:, :, 1])
    imag_part = product(spectra[:, 0], weights[:, :, 1]) + product(spectra[:, 1], weights[:, :, 0])
    return jnp.stack([real_part, imag_part], axis=1)


def weight_grads(spectra, gradients):

    def outer_product(left_part, right_part):
        return jnp.einsum("nkmi,nkmo->kmio", left_part, right_part, precision=highest)

    real_part = outer_product(spectra[:, 0], gradients[:, 0]) + outer_product(
        spectra[:, 1], gradients[:, 1]
    )
    imag_part = outer_product(spectra[:, 0], gradients[:, 1]) - outer_product(
        spectra[:, 1], gradients[:, 0]
    )
    return jnp.stack([real_part, imag_part], axis=2)


def input_grads(weights, gradients):

    def contract(right_part, left_part):
        return jnp.einsum("kmio,nkmo->nkmi", right_part, left_part, precision=highest)

    real_part = contract(weights[:, :, 0], gradients[:, 0]) + contract(
        weights[:, :, 1], gradients[:, 1]
    )
    imag_part = contract(weights[:, :, 0], gradients[:, 1]) - contract(
        weights[:, :, 1], gradients[:, 0]
    )
    return jnp.stack([real_part, imag_part], axis=1)


def gelu_tanh(values):
    return jax.nn.gelu(values, approximate=True)


def adam_update(weight, first_moment, second_moment, gradients):
    new_first = 0.9 * first_moment + 0.1 * gradients
    new_second = 0.999 * second_moment + 0.001 * gradients * gradients
    corrected_first = new_first / (1.0 - 0.9**STEP)
    corrected_second = new_second / (1.0 - 0.999**STEP)
    new_weight = weight - learning_rate * corrected_first / (jnp.sqrt(corrected_second) + 1e-08)
    return (new_weight, new_first, new_second)


def on_device(snapshots, cotangent, local_weight, spectral_weight, first_moment, second_moment):
    channels = snapshots.shape[1]
    outputs = cotangent.shape[1]
    owned_modes = spectral_weight.shape[1]
    kz_numbers = jnp.arange(KZ, dtype=jnp.int32)
    unit_scale = jnp.ones((KZ,), jnp.float32)
    fold_scale = jnp.where(kz_numbers == 0, 1.0, 2.0).astype(jnp.float32) / (NX * NY * NZ)
    forward_plain = forward_tables(unit_scale)
    forward_scaled = forward_tables(fold_scale)
    inverse_scaled = inverse_tables(fold_scale)
    inverse_plain = inverse_tables(unit_scale)
    gathered = lax.all_gather(spectral_weight, "dp", axis=0, tiled=True)
    weights = gathered.reshape(KX, owned_modes, 2, channels, outputs)
    spectra = forward_modes(snapshots, forward_plain)
    mixed = mix_modes(spectra, weights)
    local_term = jnp.einsum(
        "ncxyz,co->noxyz", snapshots, local_weight, preferred_element_type=jnp.float32
    )
    pre_act = inverse_modes(mixed, inverse_scaled) + local_term
    _, backward = jax.vjp(gelu_tanh, pre_act)
    pre_grad = backward(cotangent.astype(jnp.float32))[0].astype(jnp.bfloat16)
    local_part = jnp.einsum(
        "ncxyz,noxyz->co", snapshots, pre_grad, preferred_element_type=jnp.float32
    )
    local_grad = lax.psum(local_part, ("dp", "grid"))
    mode_grad = forward_modes(pre_grad, forward_scaled)
    summed = weight_grads(spectra, mode_grad).reshape(KX, owned_modes, -1)
    gradients = lax.psum_scatter(summed, "dp", scatter_dimension=0, tiled=True)
    input_modes = input_grads(weights, mode_grad)
    back_local = jnp.einsum(
        "noxyz,co->ncxyz", pre_grad, local_weight, preferred_element_type=jnp.float32
    )
    grad_input = (inverse_modes(input_modes, inverse_plain) + back_local).astype(jnp.bfloat16)
    new_weight, new_first, new_second = adam_update(
        spectral_weight, first_moment, second_moment, gradients
    )
    return (grad_input, local_grad, new_weight, new_first, new_second)


def solution(mesh):
    in_specs = (
        P("dp", None, "grid", None, None),
        P("dp", None, "grid", None, None),
        P(),
        P("dp", "grid", None),
        P("dp", "grid", None),
        P("dp", "grid", None),
    )
    out_specs = (
        P("dp", None, "grid", None, None),
        P(),
        P("dp", "grid", None),
        P("dp", "grid", None),
        P("dp", "grid", None),
    )
    return jax.shard_map(
        on_device, mesh=mesh, in_specs=in_specs, out_specs=out_specs, check_vma=False
    )
```

profile of v0, /device:TPU:1, one launch (start us, length us, event | category | flops | bytes accessed | tf_op | source)
XLA Modules:
  0.0 636.4 jit_solution(2044827922323537140)
XLA Ops:
  15.0 34.2 %copy.120 = f32[1,2,2,32,16,64]{2,1,5,4,3,0:T(2,128)} copy(f32[1,2,2,32,16,64]{5,3,4,2,1,0:T(8,128)S(1)} %fusion.33) | data formatting | bytes 1048576 | tf_op jit(solution)/shard_map/reshape | solution.py:65
  49.1 49.5 %reshape.1023 = f32[64,1,2048]{2,1,0:T(1,128)} reshape(f32[32768,1,2,2]{3,2,1,0:T(2,128)} %bitcast.298) | data formatting | bytes 1048576
  98.6 12.8 %all-to-all-start = ((f32[64,1,2048]{2,1,0:T(1,128)}), f32[64,1,2048]{2,1,0:T(1,128)S(1)}, u32[]{:S(2)}, u32[]{:S(2)}) async-start(f32[64,1,2048]{2,1,0:T(1,128)} %reshape.1023), calls=%async_computation | async-start | bytes 1048576 | tf_op jit(solution)/shard_map/all_to_all | solution.py:66
  112.7 15.9 %all-to-all-done = f32[64,1,2048]{2,1,0:T(1,128)S(1)} async-done(((f32[64,1,2048]{2,1,0:T(1,128)}), f32[64,1,2048]{2,1,0:T(1,128)S(1)}, u32[]{:S(2)}, u32[]{:S(2)}) %all-to-all-start) | async-done | bytes 524320 | tf_op jit(solution)/shard_map/all_to_all | solution.py:66
  131.0 53.4 %reshape.1024 = f32[32768,1,2,2]{3,2,1,0:T(2,128)} reshape(f32[64,2048]{1,0:T(8,128)S(1)} %reduce) | data formatting | bytes 1048576
  184.5 36.6 %copy.62 = f32[1,2,2,64,512]{4,2,3,1,0:T(2,128)} copy(f32[1,2,2,64,512]{2,1,4,3,0:T(2,128)} %bitcast.299) | data formatting | bytes 1048576 | tf_op jit(solution)/shard_map/all_to_all | solution.py:66
  226.5 10.8 %reshape.966 = f32[32,8,2,64,32]{4,3,2,1,0:T(8,128)} reshape(f32[32,8,4096]{2,1,0:T(8,128)} %all-gather.2.cloned.1.call-done) | data formatting | bytes 8388608 | tf_op jit(solution)/shard_map/reshape | solution.py:150
  237.3 9.6 %fusion.3 = f32[32,8,1,32]{3,2,1,0:T(1,128)S(1)} fusion(f32[32,8,2,64,32]{4,3,2,1,0:T(8,128)} %reshape.966, f32[32,8,64,1]{2,0,1,3:T(8,128)S(1)} %get-tuple-element.11), kind=kOutput, calls=%fused_computation.8 | convolution fusion | flops 6291456 | bytes 8486912 | tf_op jit(solution)/shard_map/nkmi,kmio->nkmo/dot_general | solution.py:90
  246.9 10.0 %fusion.6 = f32[32,8,1,32]{3,2,1,0:T(1,128)S(1)} fusion(f32[32,8,2,64,32]{4,3,2,1,0:T(8,128)} %reshape.966, f32[32,8,64,1]{2,0,1,3:T(8,128)S(1)} %get-tuple-element.11), kind=kOutput, calls=%fused_computation.11 | convolution fusion | flops 6291456 | bytes 8486912 | tf_op jit(solution)/shard_map/nkmi,kmio->nkmo/dot_general | solution.py:90
  264.1 7.4 %fusion.2 = f32[32,8,1,32]{3,2,1,0:T(1,128)S(1)} fusion(f32[32,8,2,64,32]{4,3,2,1,0:T(8,128)S(1)} %copy-done.1, f32[32,8,64,1]{2,0,1,3:T(8,128)S(1)} %get-tuple-element.12), kind=kOutput, calls=%fused_computation.7 | convolution fusion | flops 6291456 | bytes 8552448 | tf_op jit(solution)/shard_map/nkmi,kmio->nkmo/dot_general | solution.py:90
  281.3 7.5 %all-to-all-done.1 = f32[1,2,128,256]{3,1,0,2:T(2,128)S(1)} async-done(((f32[1,2,128,256]{3,1,0,2:T(2,128)}), f32[1,2,128,256]{3,1,0,2:T(2,128)S(1)}, u32[]{:S(2)}, u32[]{:S(2)}) %all-to-all-start.1) | async-done | bytes 262176 | tf_op jit(solution)/shard_map/all_to_all | solution.py:79
  305.0 20.9 %copy.121 = f32[1,2,2,32,16,32]{2,1,5,4,3,0:T(2,128)} copy(f32[1,2,2,32,16,32]{5,3,4,2,1,0:T(8,128)} %convolution_bitcast_fusion.1) | data formatting | bytes 524288 | tf_op jit(solution)/shard_map/reshape | solution.py:65
  326.0 25.9 %reshape.1025 = f32[64,1,1024]{2,1,0:T(1,128)} reshape(f32[16384,1,2,2]{3,2,1,0:T(2,128)} %bitcast.300) | data formatting | bytes 524288
  359.9 9.0 %all-to-all-done.2 = f32[64,1,1024]{2,1,0:T(1,128)} async-done(((f32[64,1,1024]{2,1,0:T(1,128)}), f32[64,1,1024]{2,1,0:T(1,128)}, u32[]{:S(2)}, u32[]{:S(2)}) %all-to-all-start.2) | async-done | bytes 262176 | tf_op jit(solution)/shard_map/all_to_all | solution.py:66
  371.1 27.0 %reshape.1026 = f32[16384,1,2,2]{3,2,1,0:T(2,128)} reshape(f32[64,1024]{1,0:T(8,128)S(1)} %reduce.1) | data formatting | bytes 524288
  398.2 17.9 %copy.73 = f32[1,2,2,64,256]{4,2,3,1,0:T(2,128)S(1)} copy(f32[1,2,2,64,256]{2,1,4,3,0:T(2,128)} %bitcast.301) | data formatting | bytes 524288 | tf_op jit(solution)/shard_map/all_to_all | solution.py:66
  432.4 13.0 %reshape.979 = f32[32,8,4096]{2,1,0:T(8,128)} reshape(f32[32,8,2,64,32]{4,3,2,1,0:T(8,128)} %pad_maximum_fusion) | data formatting | bytes 8388608 | tf_op jit(solution)/shard_map/reshape | solution.py:164
  445.4 15.4 %fusion.5 = f32[32,8,1,64]{3,2,1,0:T(1,128)S(1)} fusion(f32[32,8,2,64,32]{4,3,2,1,0:T(8,128)} %reshape.966, f32[32,8,32,1]{2,0,1,3:T(8,128)S(1)} %get-tuple-element.16), kind=kOutput, calls=%fused_computation.10 | convolution fusion | flops 6291456 | bytes 8486912 | tf_op jit(solution)/shard_map/kmio,nkmo->nkmi/dot_general | solution.py:114
  460.9 15.7 %fusion.1 = f32[32,8,1,64]{3,2,1,0:T(1,128)S(1)} fusion(f32[32,8,2,64,32]{4,3,2,1,0:T(8,128)} %reshape.966, f32[32,8,32,1]{2,0,1,3:T(8,128)S(1)} %get-tuple-element.15), kind=kOutput, calls=%fused_computation.6 | convolution fusion | flops 6291456 | bytes 8486912 | tf_op jit(solution)/shard_map/kmio,nkmo->nkmi/dot_general | solution.py:114
  476.6 15.4 %fusion.4 = f32[32,8,1,64]{3,2,1,0:T(1,128)S(1)} fusion(f32[32,8,2,64,32]{4,3,2,1,0:T(8,128)} %reshape.966, f32[32,8,32,1]{2,0,1,3:T(8,128)S(1)} %get-tuple-element.15), kind=kOutput, calls=%fused_computation.9 | convolution fusion | flops 6291456 | bytes 8486912 | tf_op jit(solution)/shard_map/kmio,nkmo->nkmi/dot_general | solution.py:114
  492.0 15.6 %fusion = f32[32,8,1,64]{3,2,1,0:T(1,128)S(1)} fusion(f32[32,8,2,64,32]{4,3,2,1,0:T(8,128)} %reshape.966, f32[32,8,32,1]{2,0,1,3:T(8,128)S(1)} %get-tuple-element.16), kind=kOutput, calls=%fused_computation.5 | convolution fusion | flops 6291456 | bytes 8486912 | tf_op jit(solution)/shard_map/kmio,nkmo->nkmi/dot_general | solution.py:114
  510.4 7.9 %all-to-all-start.3 = ((f32[1,2,128,512]{3,1,0,2:T(2,128)}), f32[1,2,128,512]{3,1,0,2:T(2,128)}, u32[]{:S(2)}, u32[]{:S(2)}) async-start(f32[1,2,128,512]{3,1,0,2:T(2,128)} %copy.75), calls=%async_computation.3 | async-start | bytes 1048576 | tf_op jit(solution)/shard_map/all_to_all | solution.py:79
  520.6 78.7 %psum.7 = f32[64,32]{0,1:T(8,128)} all-reduce(f32[64,32]{0,1:T(8,128)S(1)} %fusion.36), channel_id=1, replica_groups=mesh['dp'=4,'grid'=64] {'dp','grid'}, use_global_device_ids=true, to_apply=%region_0.1 | all-reduce | flops 2048 | bytes 16384 | tf_op jit(solution)/shard_map/psum | solution.py:162
  612.5 12.6 %fusion.32 = bf16[1,64,2,64,128]{4,3,2,1,0:T(8,128)(2,1)} fusion(f32[2,64,128,64]{2,3,1,0:T(8,128)} %fusion.49, f32[64,2,64,2,16]{2,4,3,1,0:T(8,128)} %copy.78, f32[1,16,128]{2,1,0:T(8,128)S(1)} %get-tuple-element.44, f32[1,16,128]{2,1,0:T(8,128)S(1)} %get-tuple-element.45), kind=kOutput, calls=%fused_computation.41 | convolution fusion | flops 404754432 | bytes 7356416 | tf_op jit(solution)/shard_map/noxysq,sqz->noxyz/dot_general | solution.py:84
  (104 shorter events, 98.5 us)
Async XLA Ops:
  7.2 1.6 copy-start
  7.2 219.4 %all-gather.2.cloned.1.call-start = ((), (), s32[]{:S(2)}) async-start(), calls=%async_computation.5 | async-start | bytes 5242880 | tf_op jit(solution)/shard_map/all_gather | solution.py:149
  98.6 30.0 %all-to-all-start = ((f32[64,1,2048]{2,1,0:T(1,128)}), f32[64,1,2048]{2,1,0:T(1,128)S(1)}, u32[]{:S(2)}, u32[]{:S(2)}) async-start(f32[64,1,2048]{2,1,0:T(1,128)} %reshape.1023), calls=%async_computation | async-start | bytes 1048576 | tf_op jit(solution)/shard_map/all_to_all | solution.py:66
  111.7 112.2 %copy-start.11 = (f32[1,2,128,32]{2,3,0,1:T(8,128)}, f32[1,2,128,32]{2,3,0,1:T(8,128)S(1)}, u32[]{:S(2)}) copy-start(f32[1,2,128,32]{2,3,0,1:T(8,128)S(1)} %get-tuple-element.22) | copy-start | bytes 98308
  111.7 112.2 %copy-start.12 = (f32[1,2,128,32]{2,3,0,1:T(8,128)}, f32[1,2,128,32]{2,3,0,1:T(8,128)S(1)}, u32[]{:S(2)}) copy-start(f32[1,2,128,32]{2,3,0,1:T(8,128)S(1)} %get-tuple-element.23) | copy-start | bytes 98308
  111.8 159.9 %copy-start.9 = (f32[1,2,32,128]{3,2,0,1:T(8,128)}, f32[1,2,32,128]{3,2,0,1:T(8,128)S(1)}, u32[]{:S(2)}) copy-start(f32[1,2,32,128]{3,2,0,1:T(8,128)S(1)} %get-tuple-element.20) | copy-start | bytes 98308
  111.9 159.9 %copy-start.10 = (f32[1,2,32,128]{3,2,0,1:T(8,128)}, f32[1,2,32,128]{3,2,0,1:T(8,128)S(1)}, u32[]{:S(2)}) copy-start(f32[1,2,32,128]{3,2,0,1:T(8,128)S(1)} %get-tuple-element.21) | copy-start | bytes 98308
  112.0 178.6 %copy-start.5 = (f32[1,2,32,64]{3,2,0,1:T(8,128)}, f32[1,2,32,64]{3,2,0,1:T(8,128)S(1)}, u32[]{:S(2)}) copy-start(f32[1,2,32,64]{3,2,0,1:T(8,128)S(1)} %get-tuple-element.18) | copy-start | bytes 49156
  112.0 178.6 %copy-start.7 = (f32[1,2,32,64]{3,2,0,1:T(8,128)}, f32[1,2,32,64]{3,2,0,1:T(8,128)S(1)}, u32[]{:S(2)}) copy-start(f32[1,2,32,64]{3,2,0,1:T(8,128)S(1)} %get-tuple-element.19) | copy-start | bytes 49156
  237.3 19.6 %copy-start.1 = (f32[32,8,2,64,32]{4,3,2,1,0:T(8,128)S(1)}, f32[32,8,2,64,32]{4,3,2,1,0:T(8,128)}, u32[]{:S(2)}) copy-start(f32[32,8,2,64,32]{4,3,2,1,0:T(8,128)} %reshape.966) | copy-start | bytes 12582916
  264.1 14.4 %copy-start.13 = (bf16[64,32]{0,1:T(8,128)(2,1)S(1)}, bf16[64,32]{0,1:T(8,128)(2,1)}, u32[]{:S(2)}) copy-start(bf16[64,32]{0,1:T(8,128)(2,1)} %param.8) | copy-start | bytes 12292
  273.1 15.8 %all-to-all-start.1 = ((f32[1,2,128,256]{3,1,0,2:T(2,128)}), f32[1,2,128,256]{3,1,0,2:T(2,128)S(1)}, u32[]{:S(2)}, u32[]{:S(2)}) async-start(f32[1,2,128,256]{3,1,0,2:T(2,128)} %copy.64), calls=%async_computation.1 | async-start | bytes 524288 | tf_op jit(solution)/shard_map/all_to_all | solution.py:79
  289.2 3.7 copy-start.14
  289.2 3.7 copy-start.15
  326.0 33.1 %copy-start.4 = (f32[32,8,64]{2,0,1:T(8,128)S(1)}, f32[32,8,64]{2,0,1:T(8,128)}, u32[]{:S(2)}) copy-start(f32[32,8,64]{2,0,1:T(8,128)} %get-tuple-element.10) | copy-start | bytes 196612
  326.0 33.2 %copy-start.3 = (f32[32,8,64]{2,0,1:T(8,128)S(1)}, f32[32,8,64]{2,0,1:T(8,128)}, u32[]{:S(2)}) copy-start(f32[32,8,64]{2,0,1:T(8,128)} %get-tuple-element.13) | copy-start | bytes 196612
  351.9 17.1 %all-to-all-start.2 = ((f32[64,1,1024]{2,1,0:T(1,128)}), f32[64,1,1024]{2,1,0:T(1,128)}, u32[]{:S(2)}, u32[]{:S(2)}) async-start(f32[64,1,1024]{2,1,0:T(1,128)} %reshape.1025), calls=%async_computation.2 | async-start | bytes 524288 | tf_op jit(solution)/shard_map/all_to_all | solution.py:66
  358.6 266.6 %reduce-scatter.2.cloned.1.call-start = ((), (), s32[]{:S(2)}) async-start(), calls=%async_computation.6 | async-start | bytes 5242880 | tf_op jit(solution)/shard_map/reduce_scatter | solution.py:165
  510.4 91.7 %all-to-all-start.3 = ((f32[1,2,128,512]{3,1,0,2:T(2,128)}), f32[1,2,128,512]{3,1,0,2:T(2,128)}, u32[]{:S(2)}, u32[]{:S(2)}) async-start(f32[1,2,128,512]{3,1,0,2:T(2,128)} %copy.75), calls=%async_computation.3 | async-start | bytes 1048576 | tf_op jit(solution)/shard_map/all_to_all | solution.py:79
  520.6 84.8 %copy-start.6 = (f32[1,2,32,64]{3,2,0,1:T(8,128)S(1)}, f32[1,2,32,64]{3,2,0,1:T(8,128)}, u32[]{:S(2)}) copy-start(f32[1,2,32,64]{3,2,0,1:T(8,128)} %copy-done.5) | copy-start | bytes 49156
  520.6 84.8 %copy-start.8 = (f32[1,2,32,64]{3,2,0,1:T(8,128)S(1)}, f32[1,2,32,64]{3,2,0,1:T(8,128)}, u32[]{:S(2)}) copy-start(f32[1,2,32,64]{3,2,0,1:T(8,128)} %copy-done.7) | copy-start | bytes 49156
  612.5 12.6 %copy-start.2 = (f32[8,8,4096]{2,1,0:T(8,128)S(1)}, f32[8,8,4096]{2,1,0:T(8,128)}, u32[]{:S(2)}) copy-start(f32[8,8,4096]{2,1,0:T(8,128)} %param.9) | copy-start | bytes 3145732
Sparse Core Ops, SparseCore 0:
  9.8 70.7 all-gather.1
  445.5 81.3 reduce-scatter.1
where the time goes:
time: 647 us; the launch traced here: 636 us
  local copies, waits for them, and re-layouts  309 us (48%)
  matrix products  146 us (23%)
  blocking collectives  78.7 us (12%)
  starting transfers between devices  33.3 us (5%)
  waiting for transfers between devices  33.2 us (5%)
  other arithmetic  21.2 us (3%)
  between operations  14.9 us (2%)
    unnamed x36, local copies, waits for them, and re-layouts  157 us
    psum x1, blocking collectives, on_device(): local_grad = lax.psum(local_part, ('dp', 'grid'))  78.7 us
    dot_general x4, matrix products, contract(): jnp.einsum('kmio,nkmo->nkmi', right_part, left_part, precision=highest)  62.2 us
    reshape x2, local copies, waits for them, and re-layouts, forward_modes(): partial_y.reshape(snapshot_count, 2, slab_width, KY * KZ * channel_count)  55.1 us
    all_to_all x3, local copies, waits for them, and re-layouts, forward_modes(): lax.all_to_all(flattened, 'grid', split_axis=3, concat_axis=2, tiled=True)  55 us
    dot_general x4, matrix products, product(): jnp.einsum('nkmi,kmio->nkmo', left_part, right_part, precision=highest)  34.2 us
    all_to_all x2, waiting for transfers between devices, forward_modes(): lax.all_to_all(flattened, 'grid', split_axis=3, concat_axis=2, tiled=True)  25 us
    dot_general x2, matrix products, inverse_modes(): return jnp.einsum('noxysq,sqz->noxyz', along_y, z_table, precision=highest)  19.6 us
  transfers between devices with their start and end apart: 6, of which 3 were waited for; matrix products, arithmetic and copies ran while one was open for 45% of the time, Pallas kernels for 0%

commit v1 on v0

v1 whole, which is shorter than its diff:
```python
import math

import jax
import jax.numpy as jnp
import ml_dtypes
import numpy as np
from jax import lax
from jax.experimental import pallas as pl
from jax.experimental.pallas import tpu as pltpu
from jax.sharding import PartitionSpec as P

NX = 128
NY = 64
NZ = 128
KX = 32
KY = 32
KZ = 16
STEP = 100
C = 64
CO = 32
GRID = 64
DP = 4
RATE = 0.02

MESH = pl.DeviceIdType.MESH
F32 = jnp.float32
BF16 = jnp.bfloat16
NN = (((1,), (0,)), ((), ()))
NT = (((1,), (1,)), ((), ()))


def mode_numbers(length, retained):
    a = np.arange(retained)
    return np.where(a < retained // 2, a, length - retained + a)


def angles(length, numbers):
    points = np.arange(length)
    return (points[:, None] * numbers[None, :] % length) * (2.0 * math.pi / length)


def rotation(theta, direction):
    cos, sin = np.cos(theta), direction * np.sin(theta)
    return np.stack([np.stack([cos, sin]), np.stack([-sin, cos])])


def split_table(table):
    high = table.astype(ml_dtypes.bfloat16)
    low = (table - high.astype(np.float64)).astype(ml_dtypes.bfloat16)
    return np.stack([high, low])


def make_tables():
    z_angles = angles(NZ, np.arange(KZ))
    fold = np.where(np.arange(KZ) == 0, 1.0, 2.0) / (NX * NY * NZ)
    z_fwd = np.concatenate([np.cos(z_angles).T, -np.sin(z_angles).T]).astype(ml_dtypes.bfloat16)
    z_fwd_scaled = (z_fwd.astype(np.float64) * np.tile(fold, 2)[:, None]).astype(ml_dtypes.bfloat16)
    z_inv = np.concatenate([np.cos(z_angles).T, -np.sin(z_angles).T])
    z_inv_scaled = z_inv * np.tile(fold, 2)[:, None]

    def four(table):
        out = np.zeros((4, 2 * KZ, 4, NZ))
        for j in range(4):
            out[j, :, j] = table
        return split_table(out.reshape(4 * 2 * KZ, 4 * NZ))

    y_theta = angles(NY, mode_numbers(NY, KY))
    x_theta = angles(NX, mode_numbers(NX, KX))
    y_rot = rotation(y_theta, -1.0)
    x_rot = rotation(x_theta, -1.0)
    x_rot = x_rot.reshape(2, 2, GRID, 2, DP, KX // DP)
    yi_rot = rotation(y_theta.T, 1.0)
    xi_rot = rotation(x_theta.T, 1.0)
    xi_rot = xi_rot.reshape(2, 2, DP, KX // DP, GRID, 2)
    y_fwd = np.zeros((KY, 2, 2, 2, 2, 2, 2, NY))
    x_fwd = np.zeros((DP, 2, 2, 8, GRID, 2, 2, 2))
    x_inv = np.zeros((GRID, 2, 2, 2, DP, 2, 2, 8))
    y_inv = np.zeros((KY, 2, 2, 2, 2, 2, 2, NY))
    for c in range(2):
        x_fwd[:, c, :, :, :, c] = x_rot.transpose(4, 1, 5, 2, 3, 0)
        x_inv[:, c, :, :, :, c] = xi_rot.transpose(4, 5, 1, 2, 0, 3)
        for x in range(2):
            y_fwd[:, c, x, :, c, :, x] = y_rot.transpose(3, 1, 0, 2)
            y_inv[:, c, x, :, c, :, x] = yi_rot.transpose(2, 0, 1, 3)
    spread = np.zeros((8, 16, 8, 16, 32))
    for q in range(8):
        for c in range(16):
            spread[q, c, q, c] = 1.0
    gather = np.zeros((8, 4, 32, 32, 8))
    for q in range(8):
        for o in range(32):
            gather[q, :, o, o, q] = 1.0
    return (
        z_fwd,
        z_fwd_scaled,
        four(z_inv_scaled),
        four(z_inv),
        split_table(y_fwd.reshape(256, 512)),
        split_table(x_fwd.reshape(128, 512)),
        split_table(x_inv.reshape(512, 128)),
        split_table(y_inv.reshape(256, 512)),
        spread.reshape(8, 128, 512).astype(ml_dtypes.bfloat16),
        gather.reshape(1024, 256).astype(ml_dtypes.bfloat16),
    )


def dot(a, b, dims=NN):
    return lax.dot_general(a, b, dims, preferred_element_type=F32)


def split(a):
    high = a.astype(BF16)
    return high, (a - high.astype(F32)).astype(BF16)


def table_dot(table, values, dims=NN):
    high, low = split(values)
    return dot(table[0], high, dims) + dot(table[0], low, dims) + dot(table[1], high, dims)


def dot_table(values, table):
    high, low = split(values)
    return dot(high, table[0]) + dot(low, table[0]) + dot(high, table[1])


def dot_exact(values, table, dims=NN):
    high, low = split(values)
    return dot(high, table, dims) + dot(low, table, dims)


def kernel(
    snap, cot, lw, weight_hbm, first_hbm, second_hbm,
    z_fwd, z_fwd_scaled, z_inv_scaled, z_inv, y_fwd, x_fwd, x_inv, y_inv, spread, gather,
    out, local_out, new_weight_hbm, new_first_hbm, new_second_hbm,
    weight, first, second, new_weight, new_first, new_second,
    zb, snap_f, pre, back, grad_b, grad_f, ub, spec_x, mixed, grad_x,
    send1, recv1, send2, recv2, send3, recv3, send4, recv4,
    dsend1, drecv1, dsend2, drecv2, dsend3, drecv3, dsend4, drecv4,
    lsend, lrecv, send_sems, recv_sems, state_sems,
):
    d = lax.axis_index("dp")
    me = lax.axis_index("grid")
    slot_of = lambda g: (g % 2) * 32 + g // 2

    def load_state(i, _):
        lanes = pl.ds(pl.multiple_of(i * 128, 128), 128)
        for n, (src, dst) in enumerate(((weight_hbm, weight), (first_hbm, first), (second_hbm, second))):
            pltpu.make_async_copy(src.at[:, lanes], dst.at[i], state_sems.at[n]).start()
        return 0

    lax.fori_loop(0, 32, load_state, 0)

    barrier = pltpu.get_barrier_semaphore()

    def greet_grid(i, _):
        pl.semaphore_signal(barrier, inc=1, device_id={"grid": (me + i) % GRID}, device_id_type=MESH)
        return 0

    def greet_dp(i, _):
        pl.semaphore_signal(barrier, inc=1, device_id={"dp": (d + i) % DP}, device_id_type=MESH)
        return 0

    lax.fori_loop(1, GRID, greet_grid, 0)
    lax.fori_loop(1, DP, greet_dp, 0)

    def grid_send(n, src, dst, src_slot, dst_slot):
        def body(i, _):
            to = (me + i) % GRID
            pltpu.make_async_remote_copy(
                src_ref=src.at[src_slot(to)],
                dst_ref=dst.at[dst_slot(me)],
                send_sem=send_sems.at[n],
                recv_sem=recv_sems.at[n],
                device_id={"grid": to},
                device_id_type=MESH,
            ).start()
            return 0

        lax.fori_loop(1, GRID, body, 0)
        dst[dst_slot(me)] = src[src_slot(me)]

    def dp_send(n, src, dst):
        def body(i, _):
            to = (d + i) % DP
            pltpu.make_async_remote_copy(
                src_ref=src.at[to],
                dst_ref=dst.at[d],
                send_sem=send_sems.at[n],
                recv_sem=recv_sems.at[n],
                device_id={"dp": to},
                device_id_type=MESH,
            ).start()
            return 0

        lax.fori_loop(1, DP, body, 0)
        dst[d] = src[d]

    def wait_all(sems, n, ref):
        part = ref.at[pl.ds(0, ref.shape[0] - 1)]
        pltpu.make_async_copy(part, part, sems.at[n]).wait()

    place = lambda g: g

    def forward_zy(field, table, channels, send):
        half = channels // 2

        def body(i, _):
            values = field[pl.ds(i * 1024, 1024), :]
            z = dot(table[...], values, NT)
            c = i // (half // 8)
            row = (i % (half // 8)) * 64
            for r in range(2):
                for h in range(2):
                    for j in range(8):
                        zb[c * 2 + r, pl.ds(row + h * half * 8 + j * 8, 8), :] = z[
                            (r * 2 + h) * 8 : (r * 2 + h + 1) * 8, j * 128 : (j + 1) * 128
                        ]
            return 0

        lax.fori_loop(0, channels // 8, body, 0)
        rows = half * 8
        for h in range(2):
            values = jnp.concatenate([zb[j, h * rows : (h + 1) * rows, :] for j in range(4)], axis=1)
            result = table_dot(y_fwd, values, NT)
            send[h * 32 : (h + 1) * 32] = result.reshape(32, 8, rows)

    def forward_x(recv, send):
        lanes = recv.shape[2]
        result = table_dot(x_fwd, recv[...].reshape(512, lanes))
        send[...] = result.reshape(DP, 32, lanes)

    def inverse_x(recv, send):
        lanes = recv.shape[2]
        result = table_dot(x_inv, recv[...].reshape(128, lanes))
        send[...] = result.reshape(GRID, 8, lanes)

    def inverse_y(recv):
        lanes = recv.shape[2]
        for h in range(2):
            values = recv[h * 32 : (h + 1) * 32].reshape(256, lanes).T
            result = dot_table(values, y_inv)
            for j in range(4):
                ub[j, h * lanes : (h + 1) * lanes, :] = result[:, j * 128 : (j + 1) * 128]

    def inverse_z(table, channels, finish):
        lanes = channels * 4

        def body(i, _):
            c = i // (channels // 8)
            row = (i % (channels // 8)) * 32
            parts = [
                ub[c * 2 + s, pl.ds(row + h * lanes + j * 8, 8), :]
                for j in range(4) for s in range(2) for h in range(2)
            ]
            values = jnp.concatenate(parts, axis=0).T
            result = dot_table(values, table)
            for j in range(4):
                finish(pl.ds(i * 512 + j * 128, 128), result[:, j * 128 : (j + 1) * 128])
            return 0

        lax.fori_loop(0, channels // 4, body, 0)

    forward_zy(snap, z_fwd, C, send1)
    pl.semaphore_wait(barrier, GRID - 1 + DP - 1)
    grid_send(0, send1, recv1, slot_of, place)

    def widen(i, _):
        rows = pl.ds(i * 512, 512)
        snap_f[rows, :] = snap[rows, :].astype(F32)
        return 0

    lax.fori_loop(0, 16, widen, 0)
    lw_t = lw[...].astype(F32).T.astype(BF16)

    def strided(ref, cell, channels):
        return jnp.concatenate(
            [ref[pl.ds(cell * 4 + j, channels, stride=128), :] for j in range(4)], axis=1
        ).astype(BF16)

    def local_forward(i, _):
        result = dot(lw_t, strided(snap_f, i, C))
        for j in range(4):
            pre[pl.ds(i * 4 + j, CO, stride=128), :] = result[:, j * 128 : (j + 1) * 128]
        return 0

    lax.fori_loop(0, 32, local_forward, 0)
    wait_all(recv_sems, 0, recv1)

    forward_x(recv1, dsend1)
    dp_send(1, dsend1, drecv1)
    wait_all(recv_sems, 1, drecv1)

    spectra = drecv1[...].reshape(128, 256)
    spectra = jnp.concatenate([spectra[:, :128], spectra[:, 128:]], axis=0)
    spectra_high, spectra_low = split(spectra)

    def w_tiles(r, c, t):
        return range(r * 16 + c * 8 + t * 4, r * 16 + c * 8 + t * 4 + 4)

    def w_read(ref, q, r, c, t):
        return jnp.concatenate([ref[j, pl.ds(q, 8, stride=8), :] for j in w_tiles(r, c, t)], axis=1)

    def w_write(ref, q, r, c, t, value):
        for n, j in enumerate(w_tiles(r, c, t)):
            ref[j, pl.ds(q, 8, stride=8), :] = value[:, n * 128 : (n + 1) * 128]

    def s_rows(t, s, c, r):
        return pl.ds(((t * 4 + s) * 2 + c) * 16 + r * 8, 8)

    pltpu.make_async_copy(weight, weight, state_sems.at[0]).wait()

    def mix(q, _):
        spec_x[q] = dot(spectra_high, spread[q]) + dot(spectra_low, spread[q])
        sums = [[jnp.zeros((8, 128), F32) for _ in range(2)] for _ in range(4)]
        for c in range(2):
            for t in range(2):
                w_re = w_read(weight, q, 0, c, t)
                w_im = w_read(weight, q, 1, c, t)
                for s in range(4):
                    s_re = spec_x[q, s_rows(t, s, c, 0), :]
                    s_im = spec_x[q, s_rows(t, s, c, 1), :]
                    products = (s_re * w_re - s_im * w_im, s_re * w_im + s_im * w_re)
                    for r in range(2):
                        for j in range(4):
                            sums[s][r] = sums[s][r] + products[r][:, j * 128 : (j + 1) * 128]
        for s in range(4):
            for r in range(2):
                mixed[q, (s * 2 + r) * 8 : (s * 2 + r + 1) * 8, :] = sums[s][r]
        return 0

    lax.fori_loop(0, 8, mix, 0)
    values = jnp.concatenate([mixed[q] for q in range(8)], axis=1)
    result = dot_exact(values, gather[...])
    for c in range(2):
        dsend2[:, c * 16 : (c + 1) * 16, :] = result[:, c * 128 : (c + 1) * 128].reshape(4, 16, 128)
    dp_send(2, dsend2, drecv2)
    wait_all(recv_sems, 2, drecv2)

    inverse_x(drecv2, send2)
    grid_send(3, send2, recv2, place, slot_of)
    wait_all(recv_sems, 3, recv2)

    inverse_y(recv2)

    def through_gelu(rows, spectral):
        v = spectral + pre[rows, :]
        k = math.sqrt(2.0 / math.pi)
        square = v * v
        t = jnp.tanh(k * (v + 0.044715 * (square * v)))
        slope = 0.5 * (1.0 + t) + 0.5 * v * (1.0 - t * t) * (k * (1.0 + 3 * 0.044715 * square))
        value = (cot[rows, :].astype(F32) * slope).astype(BF16)
        grad_b[rows, :] = value
        grad_f[rows, :] = value.astype(F32)

    inverse_z(z_inv_scaled, CO, through_gelu)
    forward_zy(grad_b, z_fwd_scaled, CO, send3)
    grid_send(4, send3, recv3, slot_of, place)

    lsend[...] = jnp.zeros_like(lsend)

    def local_backward(i, total):
        g = strided(grad_f, i, CO)
        result = dot(lw[...], g)
        for j in range(4):
            back[pl.ds(i * 4 + j, C, stride=128), :] = result[:, j * 128 : (j + 1) * 128]
        return total + dot(g, strided(snap_f, i, C), NT)

    total = lax.fori_loop(0, 32, local_backward, jnp.zeros((CO, C), F32))
    gx, gz, gy = me // 16, me // 4 % 4, me % 4
    rounds = (
        (gy, lambda j: {"grid": me - gy + j}),
        (gz, lambda j: {"grid": me - 4 * gz + 4 * j}),
        (gx, lambda j: {"grid": me - 16 * gx + 16 * j}),
        (d, lambda j: {"dp": j}),
    )

    def local_send(n, value):
        mine, device = rounds[n]
        lsend[n, :, 0:C] = value

        def body(i, _):
            pltpu.make_async_remote_copy(
                src_ref=lsend.at[n],
                dst_ref=lrecv.at[n, mine],
                send_sem=send_sems.at[8 + n],
                recv_sem=recv_sems.at[8 + n],
                device_id=device((mine + i) % 4),
                device_id_type=MESH,
            ).start()
            return 0

        lax.fori_loop(1, 4, body, 0)
        lrecv[n, mine] = lsend[n]

    def local_sum(n):
        wait_all(recv_sems, 8 + n, lrecv.at[n])
        return ((lrecv[n, 0] + lrecv[n, 1]) + (lrecv[n, 2] + lrecv[n, 3]))[:, 0:C]

    local_send(0, total)
    wait_all(recv_sems, 4, recv3)

    forward_x(recv3, dsend3)
    dp_send(5, dsend3, drecv3)
    local_send(1, local_sum(0))
    wait_all(recv_sems, 5, drecv3)

    values = jnp.concatenate(
        [drecv3[:, c * 16 : (c + 1) * 16, :].reshape(64, 128) for c in range(2)], axis=1
    )
    result = dot_exact(values, gather[...], NT)
    for q in range(8):
        grad_x[q] = result[:, q * 128 : (q + 1) * 128]

    def g_tile(q, s, r):
        tile = grad_x[q, (s * 2 + r) * 8 : (s * 2 + r + 1) * 8, :]
        return jnp.concatenate([tile] * 4, axis=1)

    def input_modes(q, total):
        parts = {}
        for c in range(2):
            for t in range(2):
                w_re = w_read(weight, q, 0, c, t)
                w_im = w_read(weight, q, 1, c, t)
                for s in range(4):
                    g_re, g_im = g_tile(q, s, 0), g_tile(q, s, 1)
                    parts[t, s, c, 0] = w_re * g_re + w_im * g_im
                    parts[t, s, c, 1] = w_re * g_im - w_im * g_re
        values = jnp.concatenate(
            [parts[t, s, c, r] for t in range(2) for s in range(4) for c in range(2) for r in range(2)],
            axis=0,
        )
        return total + dot_exact(values, spread[q], NT)

    total = lax.fori_loop(0, 8, input_modes, jnp.zeros((256, 128), F32))
    for t in range(2):
        dsend4[:, :, t * 128 : (t + 1) * 128] = total[t * 128 : (t + 1) * 128].reshape(4, 32, 128)
    dp_send(6, dsend4, drecv4)
    local_send(2, local_sum(1))
    wait_all(recv_sems, 6, drecv4)

    inverse_x(drecv4, send4)
    grid_send(7, send4, recv4, place, slot_of)
    local_send(3, local_sum(2))

    pltpu.make_async_copy(first, first, state_sems.at[1]).wait()
    pltpu.make_async_copy(second, second, state_sems.at[2]).wait()

    def adam(q, _):
        for c in range(2):
            for t in range(2):
                re = im = None
                for s in range(4):
                    s_re = spec_x[q, s_rows(t, s, c, 0), :]
                    s_im = spec_x[q, s_rows(t, s, c, 1), :]
                    g_re, g_im = g_tile(q, s, 0), g_tile(q, s, 1)
                    a, b = s_re * g_re + s_im * g_im, s_re * g_im - s_im * g_re
                    re, im = (a, b) if re is None else (re + a, im + b)
                for r, g in enumerate((re, im)):
                    m = 0.9 * w_read(first, q, r, c, t) + 0.1 * g
                    v = 0.999 * w_read(second, q, r, c, t) + 0.001 * g * g
                    step = (m / (1.0 - 0.9**STEP)) / (jnp.sqrt(v / (1.0 - 0.999**STEP)) + 1e-8)
                    w_write(new_first, q, r, c, t, m)
                    w_write(new_second, q, r, c, t, v)
                    w_write(new_weight, q, r, c, t, w_read(weight, q, r, c, t) - RATE * step)
        return 0

    lax.fori_loop(0, 8, adam, 0)
    states = ((new_weight, new_weight_hbm), (new_first, new_first_hbm), (new_second, new_second_hbm))

    def store_state(i, _):
        lanes = pl.ds(pl.multiple_of(i * 128, 128), 128)
        for n, (src, dst) in enumerate(states):
            pltpu.make_async_copy(src.at[i], dst.at[:, lanes], state_sems.at[3 + n]).start()
        return 0

    lax.fori_loop(0, 32, store_state, 0)
    local_out[...] = local_sum(3).T
    wait_all(recv_sems, 7, recv4)

    inverse_y(recv4)

    def finish(rows, spectral):
        out[rows, :] = (spectral + back[rows, :]).astype(BF16)

    inverse_z(z_inv, C, finish)

    for n, ref in enumerate((send1, dsend1, dsend2, send2, send3, dsend3, dsend4, send4)):
        wait_all(send_sems, n, ref)
    for n in range(4):
        wait_all(send_sems, 8 + n, lrecv.at[n])
    for n, (src, _) in enumerate(states):
        pltpu.make_async_copy(src, src, state_sems.at[3 + n]).wait()


def on_device(tables, snapshots, cotangent, local_weight, spectral_weight, first_moment, second_moment):
    vmem = pl.BlockSpec(memory_space=pltpu.VMEM)
    hbm = pl.BlockSpec(memory_space=pl.ANY)
    shape = jax.ShapeDtypeStruct
    state = shape((64, 4096), F32)
    big, small = (GRID, 8, 256), (GRID, 8, 128)
    dbig, dsmall = (DP, 32, 256), (DP, 32, 128)
    results = pl.pallas_call(
        kernel,
        out_shape=(shape((8192, 128), BF16), shape((C, CO), F32), state, state, state),
        in_specs=[vmem] * 3 + [hbm] * 3 + [vmem] * len(tables),
        out_specs=(vmem,) * 2 + (hbm,) * 3,
        scratch_shapes=[pltpu.VMEM((32, 64, 128), F32)] * 6
        + [
            pltpu.VMEM((4, 512, 128), F32),
            pltpu.VMEM((8192, 128), F32),
            pltpu.VMEM((4096, 128), F32),
            pltpu.VMEM((8192, 128), F32),
            pltpu.VMEM((4096, 128), BF16),
            pltpu.VMEM((4096, 128), F32),
            pltpu.VMEM((4, 512, 128), F32),
            pltpu.VMEM((8, 256, 512), F32),
            pltpu.VMEM((8, 64, 128), F32),
            pltpu.VMEM((8, 64, 128), F32),
        ]
        + [pltpu.VMEM(s, F32) for s in (big, big, small, small, small, small, big, big)]
        + [pltpu.VMEM(s, F32) for s in (dbig, dbig, dsmall, dsmall, dsmall, dsmall, dbig, dbig)]
        + [
            pltpu.VMEM((4, CO, 128), F32),
            pltpu.VMEM((4, 4, CO, 128), F32),
            pltpu.SemaphoreType.DMA((12,)),
            pltpu.SemaphoreType.DMA((12,)),
            pltpu.SemaphoreType.DMA((6,)),
        ],
        compiler_params=pltpu.CompilerParams(
            collective_id=0, has_side_effects=True, vmem_limit_bytes=56 * 1024 * 1024
        ),
    )(
        snapshots.reshape(8192, 128),
        cotangent.reshape(4096, 128),
        local_weight,
        spectral_weight.reshape(64, 4096),
        first_moment.reshape(64, 4096),
        second_moment.reshape(64, 4096),
        *tables,
    )
    grad_input, local_grad, new_weight, new_first, new_second = results
    return (
        grad_input.reshape(snapshots.shape),
        local_grad,
        new_weight.reshape(spectral_weight.shape),
        new_first.reshape(spectral_weight.shape),
        new_second.reshape(spectral_weight.shape),
    )


def solution(mesh):
    tables = make_tables()
    split_spec = P("dp", "grid", None)
    field_spec = P("dp", None, "grid", None, None)

    def step(*args):
        return on_device(tables, *args)

    return jax.shard_map(
        step,
        mesh=mesh,
        in_specs=(field_spec, field_spec, P(), split_spec, split_spec, split_spec),
        out_specs=(field_spec, P(), split_spec, split_spec, split_spec),
        check_vma=False,
    )
```

time: 647 us -> 115 us (0.18); the launches traced: 636 us -> 115 us
  local copies, waits for them, and re-layouts: 309 us -> 9.68 us
  matrix products: 146 us -> 0 us
  Pallas kernels: 0 us -> 105 us
  blocking collectives: 78.7 us -> 0 us
  starting transfers between devices: 33.3 us -> 0 us
  waiting for transfers between devices: 33.2 us -> 0 us
  other arithmetic: 21.2 us -> 0 us
  between operations: 14.9 us -> 0.64 us
    unnamed x36 -> x12, local copies, waits for them, and re-layouts: 157 us -> 9.68 us
    dot_general x23 -> x0, matrix products: 146 us -> none  [the longest x4 62.2 us: contract(): jnp.einsum('kmio,nkmo->nkmi', right_part, left_part, precision=highest)]
    pallas_call x0 -> x1, Pallas kernels: none -> 105 us  [on_device(): pl.pallas_call(kernel, out_shape=(shape((8192, 128), BF16), shape((C, CO)...]
    reshape x4 -> x0, local copies, waits for them, and re-layouts: 78.9 us -> none  [the longest x2 55.1 us: forward_modes(): partial_y.reshape(snapshot_count, 2, slab_width, KY * KZ * channel_count)]
    psum x1 -> x0, blocking collectives: 78.7 us -> none  [on_device(): local_grad = lax.psum(local_part, ('dp', 'grid'))]
    all_to_all x5 -> x0, local copies, waits for them, and re-layouts: 57.1 us -> none  [the longest x3 55 us: forward_modes(): lax.all_to_all(flattened, 'grid', split_axis=3, concat_axis=2, tiled=True)]
    all_to_all x4 -> x0, starting transfers between devices: 32.8 us -> none  [the longest x2 19.5 us: forward_modes(): lax.all_to_all(flattened, 'grid', split_axis=3, concat_axis=2, tiled=True)]
    all_to_all x4 -> x0, waiting for transfers between devices: 32.5 us -> none  [the longest x2 25 us: forward_modes(): lax.all_to_all(flattened, 'grid', split_axis=3, concat_axis=2, tiled=True)]
  transfers between devices with their start and end apart: 6 -> 0, of which waited for: 3 -> 0; matrix products, arithmetic and copies ran while one was open for 45% -> 0% of each run, Pallas kernels for 0% -> 0%
where the time goes in v1:
time: 115 us
  Pallas kernels  105 us (91%)
  local copies, waits for them, and re-layouts  9.68 us (8%)
    pallas_call x1, Pallas kernels, on_device(): pl.pallas_call(kernel, out_shape=(shape((8192, 128), BF16), shape((C, CO)...  105 us
    unnamed x12, local copies, waits for them, and re-layouts  9.68 us

profile of v1, /device:TPU:1, one launch (start us, length us, event | category | flops | bytes accessed | tf_op | source)
XLA Modules:
  0.0 114.9 jit_solution(8995235890242790304)
XLA Ops:
  0.6 1.4 %copy.21.lw = bf16[64,32]{1,0:T(8,128)(2,1)} copy(bf16[64,32]{0,1:T(8,128)(2,1)} %param.18) | data formatting | bytes 8192 | tf_op args[2]
  2.0 104.6 %shard_map.191 = (bf16[8192,128]{1,0:T(8,128)(2,1)}, f32[64,32]{1,0:T(8,128)}, f32[64,4096]{1,0:T(8,128)}, f32[64,4096]{1,0:T(8,128)}, f32[64,4096]{1,0:T(8,128)}) custom-call(bf16[8192,128]{1,0:T(8,128)(2,1)} %bitcast.9, bf16[4096,128]{1,0:T(8,128)(2,1)} %bitcast.11, bf16[64,32]{1,0:T(8,128)(2,1)} %copy.21.lw, f32[64,4096]{1,0:T(8,128)} %bitcast.12, ...), custom_call_target="tpu_custom_call" | custom-call | tf_op jit(solution)/shard_map/pallas_call | solution.py:502
  106.6 1.4 %copy.22 = f32[64,32]{0,1:T(8,128)} copy(f32[64,32]{1,0:T(8,128)} %get-tuple-element.16) | data formatting | bytes 16384
  108.0 0.0 copy-start.2
  108.0 3.3 %copy.27 = bf16[1,64,2,64,128]{4,3,2,1,0:T(8,128)(2,1)} copy(bf16[1,64,2,64,128]{4,3,2,1,0:T(8,128)(2,1)} %bitcast.10) | data formatting | bytes 4194304
  111.4 0.0 copy-done.2
  111.4 0.0 copy-start.1
  111.4 0.0 copy-start
  111.4 1.0 copy.28
  112.3 0.6 copy-done.1
  113.0 1.0 copy.29
  113.9 0.0 copy-done
  113.9 1.0 copy.30
Async XLA Ops:
  108.0 3.3 %copy-start.2 = (f32[64,4096]{1,0:T(8,128)S(1)}, f32[64,4096]{1,0:T(8,128)}, u32[]{:S(2)}) copy-start(f32[64,4096]{1,0:T(8,128)} %get-tuple-element.12) | copy-start | bytes 3145732
  111.4 1.6 %copy-start.1 = (f32[64,4096]{1,0:T(8,128)S(1)}, f32[64,4096]{1,0:T(8,128)}, u32[]{:S(2)}) copy-start(f32[64,4096]{1,0:T(8,128)} %get-tuple-element.13) | copy-start | bytes 3145732
  111.4 2.6 %copy-start = (f32[64,4096]{1,0:T(8,128)S(1)}, f32[64,4096]{1,0:T(8,128)}, u32[]{:S(2)}) copy-start(f32[64,4096]{1,0:T(8,128)} %get-tuple-element.14) | copy-start | bytes 3145732

commit v2 on v1

v2 whole, which is shorter than its diff:
```python
import math

import jax
import jax.numpy as jnp
import ml_dtypes
import numpy as np
from jax import lax
from jax.experimental import pallas as pl
from jax.experimental.pallas import tpu as pltpu
from jax.sharding import PartitionSpec as P

NX = 128
NY = 64
NZ = 128
KX = 32
KY = 32
KZ = 16
STEP = 100
C = 64
CO = 32
GRID = 64
DP = 4
RATE = 0.02

MESH = pl.DeviceIdType.MESH
F32 = jnp.float32
BF16 = jnp.bfloat16
NN = (((1,), (0,)), ((), ()))
NT = (((1,), (1,)), ((), ()))


def mode_numbers(length, retained):
    a = np.arange(retained)
    return np.where(a < retained // 2, a, length - retained + a)


def angles(length, numbers):
    points = np.arange(length)
    return (points[:, None] * numbers[None, :] % length) * (2.0 * math.pi / length)


def rotation(theta, direction):
    cos, sin = np.cos(theta), direction * np.sin(theta)
    return np.stack([np.stack([cos, sin]), np.stack([-sin, cos])])


def split_table(table):
    high = table.astype(ml_dtypes.bfloat16)
    low = (table - high.astype(np.float64)).astype(ml_dtypes.bfloat16)
    return np.stack([high, low])


def make_tables():
    z_angles = angles(NZ, np.arange(KZ))
    fold = np.where(np.arange(KZ) == 0, 1.0, 2.0) / (NX * NY * NZ)
    z_fwd = np.concatenate([np.cos(z_angles).T, -np.sin(z_angles).T]).astype(ml_dtypes.bfloat16)
    z_fwd_scaled = (z_fwd.astype(np.float64) * np.tile(fold, 2)[:, None]).astype(ml_dtypes.bfloat16)
    z_inv = np.concatenate([np.cos(z_angles).T, -np.sin(z_angles).T])
    z_inv_scaled = z_inv * np.tile(fold, 2)[:, None]

    def four(table):
        out = np.zeros((4, 2 * KZ, 4, NZ))
        for j in range(4):
            out[j, :, j] = table
        return split_table(out.reshape(4 * 2 * KZ, 4 * NZ))

    y_theta = angles(NY, mode_numbers(NY, KY))
    x_theta = angles(NX, mode_numbers(NX, KX))
    y_rot = rotation(y_theta, -1.0)
    x_rot = rotation(x_theta, -1.0)
    x_rot = x_rot.reshape(2, 2, GRID, 2, DP, KX // DP)
    yi_rot = rotation(y_theta.T, 1.0)
    xi_rot = rotation(x_theta.T, 1.0)
    xi_rot = xi_rot.reshape(2, 2, DP, KX // DP, GRID, 2)
    y_fwd = np.zeros((KY, 2, 2, 2, 2, 2, 2, NY))
    x_fwd = np.zeros((DP, 2, 2, 8, GRID, 2, 2, 2))
    x_inv = np.zeros((GRID, 2, 2, 2, DP, 2, 2, 8))
    y_inv = np.zeros((KY, 2, 2, 2, 2, 2, 2, NY))
    for c in range(2):
        x_fwd[:, c, :, :, :, c] = x_rot.transpose(4, 1, 5, 2, 3, 0)
        x_inv[:, c, :, :, :, c] = xi_rot.transpose(4, 5, 1, 2, 0, 3)
        for x in range(2):
            y_fwd[:, c, x, :, c, :, x] = y_rot.transpose(3, 1, 0, 2)
            y_inv[:, c, x, :, c, :, x] = yi_rot.transpose(2, 0, 1, 3)
    spread = np.zeros((8, 16, 8, 16, 32))
    for q in range(8):
        for c in range(16):
            spread[q, c, q, c] = 1.0
    gather = np.zeros((8, 4, 32, 32, 8))
    for q in range(8):
        for o in range(32):
            gather[q, :, o, o, q] = 1.0
    return (
        z_fwd,
        z_fwd_scaled,
        four(z_inv_scaled),
        four(z_inv),
        split_table(y_fwd.reshape(256, 512)),
        split_table(x_fwd.reshape(128, 512)),
        split_table(x_inv.reshape(512, 128)),
        split_table(y_inv.reshape(256, 512)),
        spread.reshape(8, 128, 512).astype(ml_dtypes.bfloat16),
        gather.reshape(1024, 256).astype(ml_dtypes.bfloat16),
    )


def dot(a, b, dims=NN):
    return lax.dot_general(a, b, dims, preferred_element_type=F32)


def split(a):
    high = a.astype(BF16)
    return high, (a - high.astype(F32)).astype(BF16)


def table_dot(table, values, dims=NN):
    high, low = split(values)
    return dot(table[0], high, dims) + dot(table[0], low, dims) + dot(table[1], high, dims)


def dot_table(values, table):
    high, low = split(values)
    return dot(high, table[0]) + dot(low, table[0]) + dot(high, table[1])


def dot_exact(values, table, dims=NN):
    high, low = split(values)
    return dot(high, table, dims) + dot(low, table, dims)


def dp_and_grid():
    return lax.axis_index("dp"), lax.axis_index("grid")


def inverse_y(recv, table, ub):
    for h in range(2):
        values = recv[h * 32 : (h + 1) * 32].reshape(256, 128).T
        result = dot_table(values, table)
        for j in range(4):
            ub[j, h * 128 : (h + 1) * 128, :] = result[:, j * 128 : (j + 1) * 128]


def inverse_z(ub, table, finish):
    def body(i, _):
        c = lax.div(i, 4)
        row = lax.rem(i, 4) * 32
        parts = [
            ub[c * 2 + s, pl.ds(row + h * 128 + j * 8, 8), :]
            for j in range(4) for s in range(2) for h in range(2)
        ]
        values = jnp.concatenate(parts, axis=0).T
        result = dot_table(values, table)
        for j in range(4):
            finish(pl.ds(i * 512 + j * 128, 128), result[:, j * 128 : (j + 1) * 128])
        return 0

    lax.fori_loop(0, 8, body, 0)


TABLES = (
    "z_fwd", "z_fwd_scaled", "z_inv_scaled", "z_inv", "y_fwd", "x_fwd", "x_inv", "y_inv", "spread", "gather"
)


def kernel(
    snap_hbm, cot_hbm, lw_hbm, weight_hbm, first_hbm, second_hbm,
    z_fwd_hbm, z_fwd_scaled_hbm, z_inv_scaled_hbm, z_inv_hbm, y_fwd_hbm, x_fwd_hbm, x_inv_hbm, y_inv_hbm,
    spread_hbm, gather_hbm,
    last_hbm, back_hbm, half_hbm, local_out, new_weight_hbm, new_first_hbm, new_second_hbm,
    snap, cot, lw_t, z_fwd, z_fwd_scaled, z_inv_scaled, z_inv, y_fwd, x_fwd, x_inv, y_inv, spread, gather,
    weight, first, second, new_weight, new_first, new_second,
    zb, snap_f, pre, back_a, back_b, grad_b, grad_f, ub, spec_x, mixed, grad_x, half,
    gsend, grecv, dsend, drecv, lsend, lrecv,
    load_sems, state_sems, out_sems, gsend_sems, grecv_sems, dsend_sems, drecv_sems, lsend_sems, lrecv_sems,
):
    d, me = dp_and_grid()
    slot_of = lambda g: lax.rem(g, 2) * 32 + lax.div(g, 2)
    place = lambda g: g
    pending, stored = [], []

    loads = {}

    def load(name, src, dst):
        copy = pltpu.make_async_copy(src, dst, load_sems.at[len(loads)])
        copy.start()
        loads[name] = copy

    def need(*names):
        for name in names:
            loads.pop(name).wait()

    def snap_rows(t, c):
        return pl.ds(c * 4096 + t * 2048, 2048)

    def load_snap(t, c, n):
        rows = snap_rows(t, c)
        return pltpu.make_async_copy(snap_hbm.at[rows], snap.at[rows], state_sems.at[n])

    load("z_fwd", z_fwd_hbm, z_fwd)
    load_snap(0, 0, 6).start()
    load_snap(0, 1, 7).start()
    load("y_fwd", y_fwd_hbm, y_fwd)
    load_snap(1, 0, 8).start()
    load_snap(1, 1, 9).start()

    barrier = pltpu.get_barrier_semaphore()

    def greet_grid(i, _):
        pl.semaphore_signal(barrier, inc=1, device_id={"grid": lax.rem(me + i, GRID)}, device_id_type=MESH)
        return 0

    def greet_dp(i, _):
        pl.semaphore_signal(barrier, inc=1, device_id={"dp": lax.rem(d + i, DP)}, device_id_type=MESH)
        return 0

    lax.fori_loop(1, GRID, greet_grid, 0)
    lax.fori_loop(1, DP, greet_dp, 0)

    load("x_fwd", x_fwd_hbm, x_fwd)
    load("spread", spread_hbm, spread)

    def load_state(n, src, dst):
        def body(i, _):
            lanes = pl.ds(pl.multiple_of(i * 128, 128), 128)
            pltpu.make_async_copy(src.at[:, lanes], dst.at[i], state_sems.at[n]).start()
            return 0

        lax.fori_loop(0, 32, body, 0)

    def need_state(n, dst):
        pltpu.make_async_copy(dst, dst, state_sems.at[n]).wait()

    load_state(0, weight_hbm, weight)
    load("gather", gather_hbm, gather)
    load("lw", lw_hbm, lw_t)
    load("x_inv", x_inv_hbm, x_inv)
    load("y_inv", y_inv_hbm, y_inv)
    load("z_inv_scaled", z_inv_scaled_hbm, z_inv_scaled)
    load("cot", cot_hbm, cot)
    load("z_fwd_scaled", z_fwd_scaled_hbm, z_fwd_scaled)
    load_state(1, first_hbm, first)
    load_state(2, second_hbm, second)
    load("z_inv", z_inv_hbm, z_inv)

    def grid_send(n, src_slot, dst_slot):
        def body(i, _):
            to = lax.rem(me + i, GRID)
            pltpu.make_async_remote_copy(
                src_ref=gsend.at[n, src_slot(to)],
                dst_ref=grecv.at[n, dst_slot(me)],
                send_sem=gsend_sems.at[n],
                recv_sem=grecv_sems.at[n],
                device_id={"grid": to},
                device_id_type=MESH,
            ).start()
            return 0

        lax.fori_loop(1, GRID, body, 0)
        grecv[n, dst_slot(me)] = gsend[n, src_slot(me)]
        pending.append((gsend_sems, n, gsend.at[n]))

    def dp_send(n):
        def body(i, _):
            to = lax.rem(d + i, DP)
            pltpu.make_async_remote_copy(
                src_ref=dsend.at[n, to],
                dst_ref=drecv.at[n, d],
                send_sem=dsend_sems.at[n],
                recv_sem=drecv_sems.at[n],
                device_id={"dp": to},
                device_id_type=MESH,
            ).start()
            return 0

        lax.fori_loop(1, DP, body, 0)
        drecv[n, d] = dsend[n, d]
        pending.append((dsend_sems, n, dsend.at[n]))

    def wait_all(sems, n, ref):
        part = ref.at[pl.ds(0, ref.shape[0] - 1)]
        pltpu.make_async_copy(part, part, sems.at[n]).wait()

    def grid_wait(n):
        wait_all(grecv_sems, n, grecv.at[n])

    def dp_wait(n):
        wait_all(drecv_sems, n, drecv.at[n])

    def forward_z(field, row_of, table, c):
        for part in range(2):
            start = row_of(c) + part * 1024
            z = dot(table[...], field[pl.ds(start, 1024), :], NT)
            for r in range(2):
                for h in range(2):
                    for j in range(8):
                        row = h * 128 + (part * 8 + j) * 8
                        zb[c * 2 + r, row : row + 8, :] = z[
                            (r * 2 + h) * 8 : (r * 2 + h + 1) * 8, j * 128 : (j + 1) * 128
                        ]

    def forward_y(n):
        for h in range(2):
            values = jnp.concatenate([zb[j, h * 128 : (h + 1) * 128, :] for j in range(4)], axis=1)
            result = table_dot(y_fwd, values, NT)
            gsend[n, h * 32 : (h + 1) * 32] = result.reshape(32, 8, 128)

    def forward_x(n, m):
        result = table_dot(x_fwd, grecv[n].reshape(512, 128))
        dsend[m] = result.reshape(DP, 32, 128)

    def inverse_x(m, n):
        result = table_dot(x_inv, drecv[m].reshape(128, 128))
        gsend[n] = result.reshape(GRID, 8, 128)

    need("z_fwd")
    for t in range(2):
        for c in range(2):
            load_snap(t, c, 6 + t * 2 + c).wait()
            forward_z(snap, lambda c: c * 4096 + t * 2048, z_fwd, c)
        if t == 0:
            need("y_fwd")
        forward_y(t)
        if t == 0:
            pl.semaphore_wait(barrier, GRID - 1 + DP - 1)
        grid_send(t, slot_of, place)

    def widen(i, _):
        rows = pl.ds(i * 512, 512)
        snap_f[rows, :] = snap[rows, :].astype(F32)
        return 0

    lax.fori_loop(0, 16, widen, 0)

    need("x_fwd")
    for t in range(2):
        grid_wait(t)
        forward_x(t, t)
        dp_send(t)

    def w_tiles(r, c, t):
        return range(r * 16 + c * 8 + t * 4, r * 16 + c * 8 + t * 4 + 4)

    def w_read(ref, q, r, c, t):
        return jnp.concatenate([ref[j, pl.ds(q, 8, stride=8), :] for j in w_tiles(r, c, t)], axis=1)

    def w_write(ref, q, r, c, t, value):
        for n, j in enumerate(w_tiles(r, c, t)):
            ref[j, pl.ds(q, 8, stride=8), :] = value[:, n * 128 : (n + 1) * 128]

    def s_rows(t, s, c, r):
        return pl.ds(((t * 4 + s) * 2 + c) * 16 + r * 8, 8)

    def mix(t):
        high, low = split(drecv[t].reshape(128, 128))

        def body(q, _):
            spec_x[q, t * 128 : (t + 1) * 128] = dot(high, spread[q]) + dot(low, spread[q])
            if t == 0:
                sums = [[jnp.zeros((8, 128), F32) for _ in range(2)] for _ in range(4)]
            else:
                sums = [[mixed[q, (s * 2 + r) * 8 : (s * 2 + r + 1) * 8, :] for r in range(2)] for s in range(4)]
            for c in range(2):
                w_re, w_im = w_read(weight, q, 0, c, t), w_read(weight, q, 1, c, t)
                for s in range(4):
                    s_re = spec_x[q, s_rows(t, s, c, 0), :]
                    s_im = spec_x[q, s_rows(t, s, c, 1), :]
                    products = (s_re * w_re - s_im * w_im, s_re * w_im + s_im * w_re)
                    for r in range(2):
                        for j in range(4):
                            sums[s][r] = sums[s][r] + products[r][:, j * 128 : (j + 1) * 128]
            for s in range(4):
                for r in range(2):
                    mixed[q, (s * 2 + r) * 8 : (s * 2 + r + 1) * 8, :] = sums[s][r]
            return 0

        lax.fori_loop(0, 8, body, 0)

    need("spread")
    need_state(0, weight)
    for t in range(2):
        dp_wait(t)
        mix(t)
    need("gather")
    values = jnp.concatenate([mixed[q] for q in range(8)], axis=1)
    result = dot_exact(values, gather[...])
    for c in range(2):
        dsend[2, :, c * 16 : (c + 1) * 16, :] = result[:, c * 128 : (c + 1) * 128].reshape(4, 16, 128)
    dp_send(2)
    need("x_inv")
    dp_wait(2)

    inverse_x(2, 2)
    grid_send(2, place, slot_of)

    def strided(ref, cell, channels):
        return jnp.concatenate(
            [ref[pl.ds(cell * 4 + j, channels, stride=128), :] for j in range(4)], axis=1
        ).astype(BF16)

    def local_forward(i, _):
        result = dot(lw_t[...], strided(snap_f, i, C))
        for j in range(4):
            pre[pl.ds(i * 4 + j, CO, stride=128), :] = result[:, j * 128 : (j + 1) * 128]
        return 0

    need("lw")
    lax.fori_loop(0, 32, local_forward, 0)
    lw = lw_t[...].astype(F32).T.astype(BF16)
    need("y_inv", "z_inv_scaled", "cot")
    grid_wait(2)

    inverse_y(grecv.at[2], y_inv, ub)

    def through_gelu(rows, spectral):
        v = spectral + pre[rows, :]
        k = math.sqrt(2.0 / math.pi)
        square = v * v
        t = jnp.tanh(k * (v + 0.044715 * (square * v)))
        slope = 0.5 * (1.0 + t) + 0.5 * v * (1.0 - t * t) * (k * (1.0 + 3 * 0.044715 * square))
        value = (cot[rows, :].astype(F32) * slope).astype(BF16)
        grad_b[rows, :] = value
        grad_f[rows, :] = value.astype(F32)

    inverse_z(ub, z_inv_scaled, through_gelu)
    need("z_fwd_scaled")
    for c in range(2):
        forward_z(grad_b, lambda c: c * 2048, z_fwd_scaled, c)
    forward_y(3)
    grid_send(3, slot_of, place)

    lsend[...] = jnp.zeros_like(lsend)

    def local_grad(i, total):
        return total + dot(strided(grad_f, i, CO), strided(snap_f, i, C), NT)

    total = lax.fori_loop(0, 32, local_grad, jnp.zeros((CO, C), F32))
    gx, gz, gy = lax.div(me, 16), lax.rem(lax.div(me, 4), 4), lax.rem(me, 4)
    rounds = (
        (gy, lambda j: {"grid": me - gy + j}),
        (gz, lambda j: {"grid": me - 4 * gz + 4 * j}),
        (gx, lambda j: {"grid": me - 16 * gx + 16 * j}),
        (d, lambda j: {"dp": j}),
    )

    def local_send(n, value):
        mine, device = rounds[n]
        lsend[n, :, 0:C] = value

        def body(i, _):
            pltpu.make_async_remote_copy(
                src_ref=lsend.at[n],
                dst_ref=lrecv.at[n, mine],
                send_sem=lsend_sems.at[n],
                recv_sem=lrecv_sems.at[n],
                device_id=device(lax.rem(mine + i, 4)),
                device_id_type=MESH,
            ).start()
            return 0

        lax.fori_loop(1, 4, body, 0)
        lrecv[n, mine] = lsend[n]
        pending.append((lsend_sems, n, lrecv.at[n]))

    def local_sum(n):
        wait_all(lrecv_sems, n, lrecv.at[n])
        return ((lrecv[n, 0] + lrecv[n, 1]) + (lrecv[n, 2] + lrecv[n, 3]))[:, 0:C]

    local_send(0, total)
    grid_wait(3)

    forward_x(3, 3)
    dp_send(3)
    dp_wait(3)

    values = jnp.concatenate(
        [drecv[3, :, c * 16 : (c + 1) * 16, :].reshape(64, 128) for c in range(2)], axis=1
    )
    result = dot_exact(values, gather[...], NT)
    for q in range(8):
        grad_x[q] = result[:, q * 128 : (q + 1) * 128]

    def g_tile(q, s, r):
        tile = grad_x[q, (s * 2 + r) * 8 : (s * 2 + r + 1) * 8, :]
        return jnp.concatenate([tile] * 4, axis=1)

    def input_modes(t):
        def body(q, total):
            parts = {}
            for c in range(2):
                w_re, w_im = w_read(weight, q, 0, c, t), w_read(weight, q, 1, c, t)
                for s in range(4):
                    g_re, g_im = g_tile(q, s, 0), g_tile(q, s, 1)
                    parts[s, c, 0] = w_re * g_re + w_im * g_im
                    parts[s, c, 1] = w_re * g_im - w_im * g_re
            values = jnp.concatenate(
                [parts[s, c, r] for s in range(4) for c in range(2) for r in range(2)], axis=0
            )
            return total + dot_exact(values, spread[q], NT)

        total = lax.fori_loop(0, 8, body, jnp.zeros((128, 128), F32))
        dsend[4 + t] = total.reshape(4, 32, 128)

    for t in range(2):
        input_modes(t)
        dp_send(4 + t)
    local_send(1, local_sum(0))

    need_state(1, first)
    need_state(2, second)

    def adam(q, _):
        for c in range(2):
            for t in range(2):
                re = im = None
                for s in range(4):
                    s_re = spec_x[q, s_rows(t, s, c, 0), :]
                    s_im = spec_x[q, s_rows(t, s, c, 1), :]
                    g_re, g_im = g_tile(q, s, 0), g_tile(q, s, 1)
                    a, b = s_re * g_re + s_im * g_im, s_re * g_im - s_im * g_re
                    re, im = (a, b) if re is None else (re + a, im + b)
                for r, g in enumerate((re, im)):
                    m = 0.9 * w_read(first, q, r, c, t) + 0.1 * g
                    v = 0.999 * w_read(second, q, r, c, t) + 0.001 * g * g
                    step = (m / (1.0 - 0.9**STEP)) / (jnp.sqrt(v / (1.0 - 0.999**STEP)) + 1e-8)
                    w_write(new_first, q, r, c, t, m)
                    w_write(new_second, q, r, c, t, v)
                    w_write(new_weight, q, r, c, t, w_read(weight, q, r, c, t) - RATE * step)
        return 0

    lax.fori_loop(0, 4, adam, 0)
    for t in range(2):
        dp_wait(4 + t)
        inverse_x(4 + t, 4 + t)
        grid_send(4 + t, place, slot_of)
    local_send(2, local_sum(1))

    def local_backward(i, _):
        result = dot(lw, strided(grad_f, i, CO))
        for j in range(4):
            for c in range(2):
                for t, ref in enumerate((back_a, back_b)):
                    row = c * 32 + t * 16
                    ref[pl.ds(c * 2048 + i * 4 + j, 16, stride=128), :] = result[
                        row : row + 16, j * 128 : (j + 1) * 128
                    ]
        return 0

    def store(n, src, dst):
        copy = pltpu.make_async_copy(src, dst, out_sems.at[n])
        copy.start()
        stored.append(copy)

    lax.fori_loop(0, 32, local_backward, 0)
    store(0, back_b, back_hbm)
    local_send(3, local_sum(2))
    lax.fori_loop(4, 8, adam, 0)
    states = ((new_weight, new_weight_hbm), (new_first, new_first_hbm), (new_second, new_second_hbm))

    def store_state(i, _):
        lanes = pl.ds(pl.multiple_of(i * 128, 128), 128)
        for n, (src, dst) in enumerate(states):
            pltpu.make_async_copy(src.at[i], dst.at[:, lanes], state_sems.at[3 + n]).start()
        return 0

    lax.fori_loop(0, 32, store_state, 0)
    need("z_inv")
    grid_wait(4)
    inverse_y(grecv.at[4], y_inv, ub)

    def finish(rows, spectral):
        half[rows, :] = (spectral + back_a[rows, :]).astype(BF16)

    inverse_z(ub, z_inv, finish)
    store(1, half, half_hbm)
    local_out[...] = local_sum(3)
    grid_wait(5)
    store(2, grecv.at[5], last_hbm)

    for sems, n, ref in pending:
        wait_all(sems, n, ref)
    for n, (src, _) in enumerate(states):
        need_state(3 + n, src)
    for copy in stored:
        copy.wait()


def last_kernel(
    last, back_hbm, half_hbm, local, weight_hbm, first_hbm, second_hbm, y_inv, z_inv,
    out_hbm, local_out, new_weight_hbm, new_first_hbm, new_second_hbm,
    back, ub, half, half_a, weight, first, second, in_sems, out_sems,
):
    back_copy = pltpu.make_async_copy(back_hbm, back, in_sems.at[0])
    back_copy.start()
    ways = (
        (half_hbm, half_a, None),
        (weight_hbm, weight, new_weight_hbm),
        (first_hbm, first, new_first_hbm),
        (second_hbm, second, new_second_hbm),
    )
    copies = [pltpu.make_async_copy(src, via, in_sems.at[1 + n]) for n, (src, via, _) in enumerate(ways)]
    for copy in copies:
        copy.start()

    def half_out(t, src):
        return [
            pltpu.make_async_copy(
                src.at[pl.ds(c * 2048, 2048)],
                out_hbm.at[pl.ds(c * 4096 + t * 2048, 2048)],
                out_sems.at[t * 2 + c],
            )
            for c in range(2)
        ]

    local_out[...] = local[...]
    inverse_y(last, y_inv, ub)
    stores = []
    for n, (copy, (_, via, dst)) in enumerate(zip(copies, ways)):
        copy.wait()
        for out in half_out(0, via) if dst is None else [pltpu.make_async_copy(via, dst, out_sems.at[3 + n])]:
            out.start()
            stores.append(out)
    back_copy.wait()

    def finish(rows, spectral):
        half[rows, :] = (spectral + back[rows, :]).astype(BF16)

    inverse_z(ub, z_inv, finish)
    for out in half_out(1, half):
        out.start()
        stores.append(out)
    for out in stores:
        out.wait()


def on_device(tables, snapshots, cotangent, local_weight, spectral_weight, first_moment, second_moment):
    vmem = pl.BlockSpec(memory_space=pltpu.VMEM)
    hbm = pl.BlockSpec(memory_space=pl.ANY)
    shape = jax.ShapeDtypeStruct
    state = shape((64, 4096), F32)
    state_scratch = pltpu.VMEM((32, 64, 128), F32)
    sems = lambda n: pltpu.SemaphoreType.DMA((n,))
    table_scratch = [pltpu.VMEM(table.shape, BF16) for table in tables]
    params = lambda **more: pltpu.CompilerParams(
        has_side_effects=True, vmem_limit_bytes=56 * 1024 * 1024, **more
    )
    last, back, half, local_grad, new_weight, new_first, new_second = pl.pallas_call(
        kernel,
        out_shape=(
            shape((GRID, 8, 128), F32), shape((4096, 128), F32), shape((4096, 128), BF16), shape((CO, C), F32),
            state, state, state,
        ),
        in_specs=[hbm] * (6 + len(tables)),
        out_specs=(hbm,) * 3 + (vmem,) + (hbm,) * 3,
        scratch_shapes=[
            pltpu.VMEM((8192, 128), BF16),
            pltpu.VMEM((4096, 128), BF16),
            pltpu.VMEM((CO, C), BF16),
        ]
        + table_scratch
        + [state_scratch] * 6
        + [
            pltpu.VMEM((4, 256, 128), F32),
            pltpu.VMEM((8192, 128), F32),
            pltpu.VMEM((4096, 128), F32),
            pltpu.VMEM((4096, 128), F32),
            pltpu.VMEM((4096, 128), F32),
            pltpu.VMEM((4096, 128), BF16),
            pltpu.VMEM((4096, 128), F32),
            pltpu.VMEM((4, 256, 128), F32),
            pltpu.VMEM((8, 256, 512), F32),
            pltpu.VMEM((8, 64, 128), F32),
            pltpu.VMEM((8, 64, 128), F32),
            pltpu.VMEM((4096, 128), BF16),
            pltpu.VMEM((6, GRID, 8, 128), F32),
            pltpu.VMEM((6, GRID, 8, 128), F32),
            pltpu.VMEM((6, DP, 32, 128), F32),
            pltpu.VMEM((6, DP, 32, 128), F32),
            pltpu.VMEM((4, CO, 128), F32),
            pltpu.VMEM((4, 4, CO, 128), F32),
        ]
        + [sems(n) for n in (16, 10, 3, 6, 6, 6, 6, 4, 4)],
        compiler_params=params(collective_id=0),
    )(
        snapshots.reshape(8192, 128),
        cotangent.reshape(4096, 128),
        local_weight.T,
        spectral_weight.reshape(64, 4096),
        first_moment.reshape(64, 4096),
        second_moment.reshape(64, 4096),
        *tables,
    )
    named = dict(zip(TABLES, tables))
    grad_input, local_grad, new_weight, new_first, new_second = pl.pallas_call(
        last_kernel,
        out_shape=(shape((8192, 128), BF16), shape((CO, C), F32), state, state, state),
        in_specs=[vmem] + [hbm] * 2 + [vmem] + [hbm] * 3 + [vmem] * 2,
        out_specs=(hbm, vmem) + (hbm,) * 3,
        scratch_shapes=[
            pltpu.VMEM((4096, 128), F32),
            pltpu.VMEM((4, 256, 128), F32),
            pltpu.VMEM((4096, 128), BF16),
            pltpu.VMEM((4096, 128), BF16),
            pltpu.VMEM((64, 4096), F32),
            pltpu.VMEM((64, 4096), F32),
            pltpu.VMEM((64, 4096), F32),
            sems(5),
            sems(7),
        ],
        compiler_params=params(),
    )(last, back, half, local_grad, new_weight, new_first, new_second, named["y_inv"], named["z_inv"])
    return (
        grad_input.reshape(snapshots.shape),
        local_grad.T,
        new_weight.reshape(spectral_weight.shape),
        new_first.reshape(spectral_weight.shape),
        new_second.reshape(spectral_weight.shape),
    )


def solution(mesh):
    tables = make_tables()
    split_spec = P("dp", "grid", None)
    field_spec = P("dp", None, "grid", None, None)

    def step(*args):
        return on_device(tables, *args)

    return jax.shard_map(
        step,
        mesh=mesh,
        in_specs=(field_spec, field_spec, P(), split_spec, split_spec, split_spec),
        out_specs=(field_spec, P(), split_spec, split_spec, split_spec),
        check_vma=False,
    )
```

time: 115 us -> 101 us (0.88)
  local copies, waits for them, and re-layouts: 9.68 us -> 0 us
  Pallas kernels: 105 us -> 101 us
    unnamed x12 -> x0, local copies, waits for them, and re-layouts: 9.68 us -> none
    pallas_call x1 -> x2, Pallas kernels: 105 us -> 101 us  [the longest x1 92.4 us: on_device(): pl.pallas_call(kernel, out_shape=(shape((GRID, 8, 128), F32), shape((4096...]
where the time goes in v2:
time: 101 us
  Pallas kernels  101 us (100%)
    pallas_call x1, Pallas kernels, on_device(): pl.pallas_call(kernel, out_shape=(shape((GRID, 8, 128), F32), shape((4096...  92.4 us
    pallas_call x1, Pallas kernels, on_device(): pl.pallas_call(last_kernel, out_shape=(shape((8192, 128), BF16), shape((C...  8.27 us

profile of v2, /device:TPU:1, one launch (start us, length us, event | category | flops | bytes accessed | tf_op | source)
XLA Modules:
  0.0 101.3 jit_solution(18346948668397315190)
XLA Ops:
  0.6 92.4 %shard_map.191 = (f32[64,8,128]{2,1,0:T(8,128)}, f32[4096,128]{1,0:T(8,128)}, bf16[4096,128]{1,0:T(8,128)(2,1)}, f32[32,64]{1,0:T(8,128)}, f32[64,4096]{1,0:T(8,...) custom-call(bf16[8192,128]{1,0:T(8,128)(2,1)} %bitcast.11, bf16[4096,128]{1,0:T(8,128)(2,1)} %bitcast.12, ...), custom_call_target="tpu_custom_call" | custom-call | tf_op jit(solution)/shard_map/pallas_call | solution.py:646
  93.0 8.3 %shard_map.192 = (bf16[8192,128]{1,0:T(8,128)(2,1)}, f32[32,64]{1,0:T(8,128)}, f32[64,4096]{1,0:T(8,128)}, f32[64,4096]{1,0:T(8,128)}, f32[64,4096]{1,0:T(8,128)}) custom-call(f32[64,8,128]{2,1,0:T(8,128)} %get-tuple-element.17.last, f32[4096,128]{1,0:T(8,128)} %get-tuple-element.18.back_hbm, bf16[4096,128]{1,0:T(8,128)(2,1)} %get-tuple-element.19.half_hbm, ...), custom_call_target="tpu_custom_call" | custom-call | tf_op jit(solution)/shard_map/pallas_call | solution.py:693

commit v3 on v2

--- a/solution.py
+++ b/solution.py
@@ -140,21 +140,26 @@
             ub[j, h * 128 : (h + 1) * 128, :] = result[:, j * 128 : (j + 1) * 128]
 
 
-def inverse_z(ub, table, finish):
+def inverse_z(ub, table, c, finish):
     def body(i, _):
-        c = lax.div(i, 4)
-        row = lax.rem(i, 4) * 32
-        parts = [
-            ub[c * 2 + s, pl.ds(row + h * 128 + j * 8, 8), :]
-            for j in range(4) for s in range(2) for h in range(2)
-        ]
-        values = jnp.concatenate(parts, axis=0).T
-        result = dot_table(values, table)
-        for j in range(4):
-            finish(pl.ds(i * 512 + j * 128, 128), result[:, j * 128 : (j + 1) * 128])
+        groups = []
+        for g in range(2):
+            row = i * 64 + g * 32
+            parts = [
+                ub[c * 2 + s, pl.ds(row + h * 128 + j * 8, 8), :]
+                for j in range(4) for s in range(2) for h in range(2)
+            ]
+            groups.append(jnp.concatenate(parts, axis=0).T)
+        result = dot_table(jnp.concatenate(groups, axis=0), table)
+        for g in range(2):
+            for j in range(4):
+                finish(
+                    pl.ds(c * 2048 + i * 1024 + g * 512 + j * 128, 128),
+                    result[g * 128 : (g + 1) * 128, j * 128 : (j + 1) * 128],
+                )
         return 0
 
-    lax.fori_loop(0, 8, body, 0)
+    lax.fori_loop(0, 2, body, 0)
 
 
 TABLES = (
@@ -178,6 +183,18 @@
     place = lambda g: g
     pending, stored = [], []
 
+    barrier = pltpu.get_barrier_semaphore()
+
+    def greet_grid(i, _):
+        pl.semaphore_signal(barrier, inc=1, device_id={"grid": lax.rem(me + i, GRID)}, device_id_type=MESH)
+        return 0
+
+    def greet_dp(i, _):
+        pl.semaphore_signal(barrier, inc=1, device_id={"dp": lax.rem(d + i, DP)}, device_id_type=MESH)
+        return 0
+
+    lax.fori_loop(1, DP, greet_dp, 0)
+
     loads = {}
 
     def load(name, src, dst):
@@ -203,29 +220,13 @@
     load_snap(1, 0, 8).start()
     load_snap(1, 1, 9).start()
 
-    barrier = pltpu.get_barrier_semaphore()
-
-    def greet_grid(i, _):
-        pl.semaphore_signal(barrier, inc=1, device_id={"grid": lax.rem(me + i, GRID)}, device_id_type=MESH)
-        return 0
-
-    def greet_dp(i, _):
-        pl.semaphore_signal(barrier, inc=1, device_id={"dp": lax.rem(d + i, DP)}, device_id_type=MESH)
-        return 0
-
     lax.fori_loop(1, GRID, greet_grid, 0)
-    lax.fori_loop(1, DP, greet_dp, 0)
 
     load("x_fwd", x_fwd_hbm, x_fwd)
     load("spread", spread_hbm, spread)
 
     def load_state(n, src, dst):
-        def body(i, _):
-            lanes = pl.ds(pl.multiple_of(i * 128, 128), 128)
-            pltpu.make_async_copy(src.at[:, lanes], dst.at[i], state_sems.at[n]).start()
-            return 0
-
-        lax.fori_loop(0, 32, body, 0)
+        pltpu.make_async_copy(src, dst, state_sems.at[n]).start()
 
     def need_state(n, dst):
         pltpu.make_async_copy(dst, dst, state_sems.at[n]).wait()
@@ -259,22 +260,29 @@
         grecv[n, dst_slot(me)] = gsend[n, src_slot(me)]
         pending.append((gsend_sems, n, gsend.at[n]))
 
-    def dp_send(n):
-        def body(i, _):
-            to = lax.rem(d + i, DP)
-            pltpu.make_async_remote_copy(
-                src_ref=dsend.at[n, to],
-                dst_ref=drecv.at[n, d],
-                send_sem=dsend_sems.at[n],
-                recv_sem=drecv_sems.at[n],
-                device_id={"dp": to},
-                device_id_type=MESH,
-            ).start()
-            return 0
-
-        lax.fori_loop(1, DP, body, 0)
+    near = lax.div(d, 2)
+    far = 1 - near
+    core = lax.rem(d, 2)
+
+    def dp_copy(n, sem, to):
+        pltpu.make_async_remote_copy(
+            src_ref=dsend.at[n, to],
+            dst_ref=drecv.at[n, d],
+            send_sem=dsend_sems.at[sem],
+            recv_sem=drecv_sems.at[sem],
+            device_id={"dp": to},
+            device_id_type=MESH,
+        ).start()
+
+    def send_far(n):
+        for i in range(2):
+            dp_copy(n, n, far * 2 + lax.rem(core + i, 2))
+        pending.append((dsend_sems, n, dsend.at[n, pl.ds(0, 3)]))
+
+    def send_near(n):
+        dp_copy(n, 6 + n, near * 2 + 1 - core)
         drecv[n, d] = dsend[n, d]
-        pending.append((dsend_sems, n, dsend.at[n]))
+        pending.append((dsend_sems, 6 + n, dsend.at[n, pl.ds(0, 2)]))
 
     def wait_all(sems, n, ref):
         part = ref.at[pl.ds(0, ref.shape[0] - 1)]
@@ -283,8 +291,11 @@
     def grid_wait(n):
         wait_all(grecv_sems, n, grecv.at[n])
 
-    def dp_wait(n):
-        wait_all(drecv_sems, n, drecv.at[n])
+    def wait_far(n):
+        wait_all(drecv_sems, n, drecv.at[n, pl.ds(0, 3)])
+
+    def wait_near(n):
+        wait_all(drecv_sems, 6 + n, drecv.at[n, pl.ds(0, 2)])
 
     def forward_z(field, row_of, table, c):
         for part in range(2):
@@ -335,59 +346,65 @@
     for t in range(2):
         grid_wait(t)
         forward_x(t, t)
-        dp_send(t)
+        send_far(t)
+        send_near(t)
 
     def w_tiles(r, c, t):
         return range(r * 16 + c * 8 + t * 4, r * 16 + c * 8 + t * 4 + 4)
 
     def w_read(ref, q, r, c, t):
-        return jnp.concatenate([ref[j, pl.ds(q, 8, stride=8), :] for j in w_tiles(r, c, t)], axis=1)
+        return jnp.concatenate([ref[pl.ds(j * 8 + q, 8, stride=256), :] for j in w_tiles(r, c, t)], axis=1)
 
     def w_write(ref, q, r, c, t, value):
         for n, j in enumerate(w_tiles(r, c, t)):
-            ref[j, pl.ds(q, 8, stride=8), :] = value[:, n * 128 : (n + 1) * 128]
+            ref[pl.ds(j * 8 + q, 8, stride=256), :] = value[:, n * 128 : (n + 1) * 128]
 
     def s_rows(t, s, c, r):
         return pl.ds(((t * 4 + s) * 2 + c) * 16 + r * 8, 8)
 
-    def mix(t):
-        high, low = split(drecv[t].reshape(128, 128))
+    def mix(t, side):
+        high, low = split(drecv[t, pl.ds(side * 2, 2)].reshape(64, 128))
 
         def body(q, _):
-            spec_x[q, t * 128 : (t + 1) * 128] = dot(high, spread[q]) + dot(low, spread[q])
+            spectra = dot(high, spread[q]) + dot(low, spread[q])
+            spec_x[q, pl.ds(pl.multiple_of(t * 128 + side * 64, 64), 64)] = spectra
             if t == 0:
-                sums = [[jnp.zeros((8, 128), F32) for _ in range(2)] for _ in range(4)]
+                sums = [[jnp.zeros((8, 128), F32) for _ in range(2)] for _ in range(2)]
             else:
-                sums = [[mixed[q, (s * 2 + r) * 8 : (s * 2 + r + 1) * 8, :] for r in range(2)] for s in range(4)]
+                sums = [[mixed[q, side * 2 + s, r * 8 : (r + 1) * 8, :] for r in range(2)] for s in range(2)]
             for c in range(2):
                 w_re, w_im = w_read(weight, q, 0, c, t), w_read(weight, q, 1, c, t)
-                for s in range(4):
-                    s_re = spec_x[q, s_rows(t, s, c, 0), :]
-                    s_im = spec_x[q, s_rows(t, s, c, 1), :]
+                for s in range(2):
+                    row = (s * 2 + c) * 16
+                    s_re, s_im = spectra[row : row + 8], spectra[row + 8 : row + 16]
                     products = (s_re * w_re - s_im * w_im, s_re * w_im + s_im * w_re)
                     for r in range(2):
                         for j in range(4):
                             sums[s][r] = sums[s][r] + products[r][:, j * 128 : (j + 1) * 128]
-            for s in range(4):
+            for s in range(2):
                 for r in range(2):
-                    mixed[q, (s * 2 + r) * 8 : (s * 2 + r + 1) * 8, :] = sums[s][r]
+                    mixed[q, side * 2 + s, r * 8 : (r + 1) * 8, :] = sums[s][r]
             return 0
 
-        lax.fori_loop(0, 8, body, 0)
+        lax.fori_loop(0, 8, body, 0, unroll=2)
 
     need("spread")
     need_state(0, weight)
     for t in range(2):
-        dp_wait(t)
-        mix(t)
+        wait_near(t)
+        mix(t, near)
+        wait_far(t)
+        mix(t, far)
     need("gather")
-    values = jnp.concatenate([mixed[q] for q in range(8)], axis=1)
+    values = jnp.concatenate([mixed[q].reshape(64, 128) for q in range(8)], axis=1)
     result = dot_exact(values, gather[...])
     for c in range(2):
         dsend[2, :, c * 16 : (c + 1) * 16, :] = result[:, c * 128 : (c + 1) * 128].reshape(4, 16, 128)
-    dp_send(2)
+    send_far(2)
+    send_near(2)
     need("x_inv")
-    dp_wait(2)
+    wait_near(2)
+    wait_far(2)
 
     inverse_x(2, 2)
     grid_send(2, place, slot_of)
@@ -404,7 +421,7 @@
         return 0
 
     need("lw")
-    lax.fori_loop(0, 32, local_forward, 0)
+    lax.fori_loop(0, 32, local_forward, 0, unroll=4)
     lw = lw_t[...].astype(F32).T.astype(BF16)
     need("y_inv", "z_inv_scaled", "cot")
     grid_wait(2)
@@ -415,25 +432,31 @@
         v = spectral + pre[rows, :]
         k = math.sqrt(2.0 / math.pi)
         square = v * v
-        t = jnp.tanh(k * (v + 0.044715 * (square * v)))
-        slope = 0.5 * (1.0 + t) + 0.5 * v * (1.0 - t * t) * (k * (1.0 + 3 * 0.044715 * square))
-        value = (cot[rows, :].astype(F32) * slope).astype(BF16)
-        grad_b[rows, :] = value
-        grad_f[rows, :] = value.astype(F32)
-
-    inverse_z(ub, z_inv_scaled, through_gelu)
+        t = jnp.tanh(v * (k + (k * 0.044715) * square))
+        bend = v * (0.5 * k + (1.5 * k * 0.044715) * square)
+        slope = (0.5 + 0.5 * t) + bend * (1.0 - t * t)
+        grad_b[rows, :] = (cot[rows, :].astype(F32) * slope).astype(BF16)
+
     need("z_fwd_scaled")
     for c in range(2):
+        inverse_z(ub, z_inv_scaled, c, through_gelu)
         forward_z(grad_b, lambda c: c * 2048, z_fwd_scaled, c)
     forward_y(3)
     grid_send(3, slot_of, place)
 
     lsend[...] = jnp.zeros_like(lsend)
 
+    def widen_grad(i, _):
+        rows = pl.ds(i * 512, 512)
+        grad_f[rows, :] = grad_b[rows, :].astype(F32)
+        return 0
+
+    lax.fori_loop(0, 8, widen_grad, 0)
+
     def local_grad(i, total):
         return total + dot(strided(grad_f, i, CO), strided(snap_f, i, C), NT)
 
-    total = lax.fori_loop(0, 32, local_grad, jnp.zeros((CO, C), F32))
+    total = lax.fori_loop(0, 32, local_grad, jnp.zeros((CO, C), F32), unroll=4)
     gx, gz, gy = lax.div(me, 16), lax.rem(lax.div(me, 4), 4), lax.rem(me, 4)
     rounds = (
         (gy, lambda j: {"grid": me - gy + j}),
@@ -466,44 +489,74 @@
         return ((lrecv[n, 0] + lrecv[n, 1]) + (lrecv[n, 2] + lrecv[n, 3]))[:, 0:C]
 
     local_send(0, total)
+
+    def local_backward(i, _):
+        result = dot(lw, strided(grad_f, i, CO))
+        for j in range(4):
+            for c in range(2):
+                for t, ref in enumerate((back_a, back_b)):
+                    row = c * 32 + t * 16
+                    ref[pl.ds(c * 2048 + i * 4 + j, 16, stride=128), :] = result[
+                        row : row + 16, j * 128 : (j + 1) * 128
+                    ]
+        return 0
+
+    def store(n, src, dst):
+        copy = pltpu.make_async_copy(src, dst, out_sems.at[n])
+        copy.start()
+        stored.append(copy)
+
+    lax.fori_loop(0, 12, local_backward, 0, unroll=4)
     grid_wait(3)
 
     forward_x(3, 3)
-    dp_send(3)
-    dp_wait(3)
-
-    values = jnp.concatenate(
-        [drecv[3, :, c * 16 : (c + 1) * 16, :].reshape(64, 128) for c in range(2)], axis=1
-    )
-    result = dot_exact(values, gather[...], NT)
-    for q in range(8):
-        grad_x[q] = result[:, q * 128 : (q + 1) * 128]
+    send_far(3)
+    send_near(3)
+    local_send(1, local_sum(0))
+
+    def spread_gradients(side):
+        rows = pl.ds(side * 2, 2)
+        values = jnp.concatenate(
+            [drecv[3, rows, c * 16 : (c + 1) * 16, :].reshape(32, 128) for c in range(2)], axis=1
+        )
+        result = dot_exact(values, gather[...], NT)
+        for q in range(8):
+            grad_x[q, rows] = result[:, q * 128 : (q + 1) * 128].reshape(2, 16, 128)
 
     def g_tile(q, s, r):
-        tile = grad_x[q, (s * 2 + r) * 8 : (s * 2 + r + 1) * 8, :]
-        return jnp.concatenate([tile] * 4, axis=1)
-
-    def input_modes(t):
+        return jnp.concatenate([grad_x[q, s, r * 8 : (r + 1) * 8, :]] * 4, axis=1)
+
+    def input_modes(t, side):
         def body(q, total):
             parts = {}
             for c in range(2):
                 w_re, w_im = w_read(weight, q, 0, c, t), w_read(weight, q, 1, c, t)
-                for s in range(4):
-                    g_re, g_im = g_tile(q, s, 0), g_tile(q, s, 1)
+                for s in range(2):
+                    g_re, g_im = g_tile(q, side * 2 + s, 0), g_tile(q, side * 2 + s, 1)
                     parts[s, c, 0] = w_re * g_re + w_im * g_im
                     parts[s, c, 1] = w_re * g_im - w_im * g_re
             values = jnp.concatenate(
-                [parts[s, c, r] for s in range(4) for c in range(2) for r in range(2)], axis=0
+                [parts[s, c, r] for s in range(2) for c in range(2) for r in range(2)], axis=0
             )
             return total + dot_exact(values, spread[q], NT)
 
-        total = lax.fori_loop(0, 8, body, jnp.zeros((128, 128), F32))
-        dsend[4 + t] = total.reshape(4, 32, 128)
-
+        total = lax.fori_loop(0, 8, body, jnp.zeros((64, 128), F32), unroll=2)
+        dsend[4 + t, pl.ds(side * 2, 2)] = total.reshape(2, 32, 128)
+
+    wait_near(3)
+    spread_gradients(near)
     for t in range(2):
-        input_modes(t)
-        dp_send(4 + t)
-    local_send(1, local_sum(0))
+        input_modes(t, near)
+        send_near(4 + t)
+    wait_far(3)
+    spread_gradients(far)
+    for t in range(2):
+        input_modes(t, far)
+        send_far(4 + t)
+    local_send(2, local_sum(1))
+    lax.fori_loop(12, 32, local_backward, 0, unroll=4)
+    store(0, back_b, back_hbm)
+    local_send(3, local_sum(2))
 
     need_state(1, first)
     need_state(2, second)
@@ -527,42 +580,16 @@
                     w_write(new_weight, q, r, c, t, w_read(weight, q, r, c, t) - RATE * step)
         return 0
 
-    lax.fori_loop(0, 4, adam, 0)
     for t in range(2):
-        dp_wait(4 + t)
+        wait_near(4 + t)
+        wait_far(4 + t)
         inverse_x(4 + t, 4 + t)
         grid_send(4 + t, place, slot_of)
-    local_send(2, local_sum(1))
-
-    def local_backward(i, _):
-        result = dot(lw, strided(grad_f, i, CO))
-        for j in range(4):
-            for c in range(2):
-                for t, ref in enumerate((back_a, back_b)):
-                    row = c * 32 + t * 16
-                    ref[pl.ds(c * 2048 + i * 4 + j, 16, stride=128), :] = result[
-                        row : row + 16, j * 128 : (j + 1) * 128
-                    ]
-        return 0
-
-    def store(n, src, dst):
-        copy = pltpu.make_async_copy(src, dst, out_sems.at[n])
-        copy.start()
-        stored.append(copy)
-
-    lax.fori_loop(0, 32, local_backward, 0)
-    store(0, back_b, back_hbm)
-    local_send(3, local_sum(2))
-    lax.fori_loop(4, 8, adam, 0)
+    lax.fori_loop(0, 8, adam, 0)
     states = ((new_weight, new_weight_hbm), (new_first, new_first_hbm), (new_second, new_second_hbm))
 
-    def store_state(i, _):
-        lanes = pl.ds(pl.multiple_of(i * 128, 128), 128)
-        for n, (src, dst) in enumerate(states):
-            pltpu.make_async_copy(src.at[i], dst.at[:, lanes], state_sems.at[3 + n]).start()
-        return 0
-
-    lax.fori_loop(0, 32, store_state, 0)
+    for n, (src, dst) in enumerate(states):
+        store(3 + n, src, dst)
     need("z_inv")
     grid_wait(4)
     inverse_y(grecv.at[4], y_inv, ub)
@@ -570,7 +597,8 @@
     def finish(rows, spectral):
         half[rows, :] = (spectral + back_a[rows, :]).astype(BF16)
 
-    inverse_z(ub, z_inv, finish)
+    for c in range(2):
+        inverse_z(ub, z_inv, c, finish)
     store(1, half, half_hbm)
     local_out[...] = local_sum(3)
     grid_wait(5)
@@ -578,66 +606,67 @@
 
     for sems, n, ref in pending:
         wait_all(sems, n, ref)
-    for n, (src, _) in enumerate(states):
-        need_state(3 + n, src)
     for copy in stored:
         copy.wait()
 
 
 def last_kernel(
-    last, back_hbm, half_hbm, local, weight_hbm, first_hbm, second_hbm, y_inv, z_inv,
+    last_hbm, back_hbm, half_hbm, local, weight_hbm, first_hbm, second_hbm, y_inv_hbm, z_inv_hbm,
     out_hbm, local_out, new_weight_hbm, new_first_hbm, new_second_hbm,
-    back, ub, half, half_a, weight, first, second, in_sems, out_sems,
+    last, back, y_inv, z_inv, ub, half, half_a, weight, first, second, in_sems, out_sems,
 ):
-    back_copy = pltpu.make_async_copy(back_hbm, back, in_sems.at[0])
-    back_copy.start()
-    ways = (
-        (half_hbm, half_a, None),
-        (weight_hbm, weight, new_weight_hbm),
-        (first_hbm, first, new_first_hbm),
-        (second_hbm, second, new_second_hbm),
-    )
-    copies = [pltpu.make_async_copy(src, via, in_sems.at[1 + n]) for n, (src, via, _) in enumerate(ways)]
-    for copy in copies:
+    sources = (last_hbm, y_inv_hbm, z_inv_hbm, back_hbm, half_hbm, weight_hbm, first_hbm, second_hbm)
+    places = (last, y_inv, z_inv, back, half_a, weight, first, second)
+    loads = [pltpu.make_async_copy(a, b, in_sems.at[n]) for n, (a, b) in enumerate(zip(sources, places))]
+    for copy in loads:
         copy.start()
-
-    def half_out(t, src):
-        return [
-            pltpu.make_async_copy(
-                src.at[pl.ds(c * 2048, 2048)],
-                out_hbm.at[pl.ds(c * 4096 + t * 2048, 2048)],
-                out_sems.at[t * 2 + c],
-            )
-            for c in range(2)
-        ]
-
-    local_out[...] = local[...]
-    inverse_y(last, y_inv, ub)
     stores = []
-    for n, (copy, (_, via, dst)) in enumerate(zip(copies, ways)):
-        copy.wait()
-        for out in half_out(0, via) if dst is None else [pltpu.make_async_copy(via, dst, out_sems.at[3 + n])]:
-            out.start()
-            stores.append(out)
-    back_copy.wait()
+
+    def store(src, dst):
+        copy = pltpu.make_async_copy(src, dst, out_sems.at[len(stores)])
+        copy.start()
+        stores.append(copy)
 
     def finish(rows, spectral):
         half[rows, :] = (spectral + back[rows, :]).astype(BF16)
 
-    inverse_z(ub, z_inv, finish)
-    for out in half_out(1, half):
-        out.start()
-        stores.append(out)
-    for out in stores:
-        out.wait()
+    def store_half(src, t, c):
+        store(src.at[pl.ds(c * 2048, 2048)], out_hbm.at[pl.ds(c * 4096 + t * 2048, 2048)])
+
+    local_out[...] = local[...]
+    loads[0].wait()
+    loads[1].wait()
+    inverse_y(last, y_inv, ub)
+    loads[2].wait()
+    loads[3].wait()
+    inverse_z(ub, z_inv, 0, finish)
+    store_half(half, 1, 0)
+    loads[4].wait()
+    for c in range(2):
+        store_half(half_a, 0, c)
+    for copy, src, dst in zip(loads[5:], places[5:], (new_weight_hbm, new_first_hbm, new_second_hbm)):
+        copy.wait()
+        store(src, dst)
+    inverse_z(ub, z_inv, 1, finish)
+    store_half(half, 1, 1)
+    for copy in stores:
+        copy.wait()
+
+
+def to_rows(state):
+    return state.reshape(8, 8, 32, 128).transpose(0, 2, 1, 3).reshape(2048, 128)
+
+
+def from_rows(rows):
+    return rows.reshape(8, 32, 8, 128).transpose(0, 2, 1, 3).reshape(8, 8, 4096)
 
 
 def on_device(tables, snapshots, cotangent, local_weight, spectral_weight, first_moment, second_moment):
     vmem = pl.BlockSpec(memory_space=pltpu.VMEM)
     hbm = pl.BlockSpec(memory_space=pl.ANY)
     shape = jax.ShapeDtypeStruct
-    state = shape((64, 4096), F32)
-    state_scratch = pltpu.VMEM((32, 64, 128), F32)
+    state = shape((2048, 128), F32)
+    state_scratch = pltpu.VMEM((2048, 128), F32)
     sems = lambda n: pltpu.SemaphoreType.DMA((n,))
     table_scratch = [pltpu.VMEM(table.shape, BF16) for table in tables]
     params = lambda **more: pltpu.CompilerParams(
@@ -668,8 +697,8 @@
             pltpu.VMEM((4096, 128), F32),
             pltpu.VMEM((4, 256, 128), F32),
             pltpu.VMEM((8, 256, 512), F32),
-            pltpu.VMEM((8, 64, 128), F32),
-            pltpu.VMEM((8, 64, 128), F32),
+            pltpu.VMEM((8, 4, 16, 128), F32),
+            pltpu.VMEM((8, 4, 16, 128), F32),
             pltpu.VMEM((4096, 128), BF16),
             pltpu.VMEM((6, GRID, 8, 128), F32),
             pltpu.VMEM((6, GRID, 8, 128), F32),
@@ -678,42 +707,42 @@
             pltpu.VMEM((4, CO, 128), F32),
             pltpu.VMEM((4, 4, CO, 128), F32),
         ]
-        + [sems(n) for n in (16, 10, 3, 6, 6, 6, 6, 4, 4)],
+        + [sems(n) for n in (16, 10, 6, 6, 6, 12, 12, 4, 4)],
         compiler_params=params(collective_id=0),
     )(
         snapshots.reshape(8192, 128),
         cotangent.reshape(4096, 128),
         local_weight.T,
-        spectral_weight.reshape(64, 4096),
-        first_moment.reshape(64, 4096),
-        second_moment.reshape(64, 4096),
+        to_rows(spectral_weight),
+        to_rows(first_moment),
+        to_rows(second_moment),
         *tables,
     )
     named = dict(zip(TABLES, tables))
     grad_input, local_grad, new_weight, new_first, new_second = pl.pallas_call(
         last_kernel,
         out_shape=(shape((8192, 128), BF16), shape((CO, C), F32), state, state, state),
-        in_specs=[vmem] + [hbm] * 2 + [vmem] + [hbm] * 3 + [vmem] * 2,
+        in_specs=[hbm] * 3 + [vmem] + [hbm] * 5,
         out_specs=(hbm, vmem) + (hbm,) * 3,
         scratch_shapes=[
+            pltpu.VMEM((GRID, 8, 128), F32),
             pltpu.VMEM((4096, 128), F32),
+            pltpu.VMEM(named["y_inv"].shape, BF16),
+            pltpu.VMEM(named["z_inv"].shape, BF16),
             pltpu.VMEM((4, 256, 128), F32),
             pltpu.VMEM((4096, 128), BF16),
             pltpu.VMEM((4096, 128), BF16),
-            pltpu.VMEM((64, 4096), F32),
-            pltpu.VMEM((64, 4096), F32),
-            pltpu.VMEM((64, 4096), F32),
-            sems(5),
-            sems(7),
-        ],
+        ]
+        + [state_scratch] * 3
+        + [sems(8), sems(7)],
         compiler_params=params(),
     )(last, back, half, local_grad, new_weight, new_first, new_second, named["y_inv"], named["z_inv"])
     return (
         grad_input.reshape(snapshots.shape),
         local_grad.T,
-        new_weight.reshape(spectral_weight.shape),
-        new_first.reshape(spectral_weight.shape),
-        new_second.reshape(spectral_weight.shape),
+        from_rows(new_weight),
+        from_rows(new_first),
+        from_rows(new_second),
     )
 
 

time: 101 us -> 97 us (0.960)
  Pallas kernels: 101 us -> 96.2 us
    pallas_call x1, Pallas kernels: 92.4 us -> 89.6 us  [on_device(): pl.pallas_call(kernel, out_shape=(shape((GRID, 8, 128), F32), shape((4096...]
    pallas_call x1, Pallas kernels: 8.27 us -> 6.56 us  [on_device(): pl.pallas_call(last_kernel, out_shape=(shape((8192, 128), BF16), shape((C...]
where the time goes in v3:
time: 97 us; the launch traced here: 96.8 us
  Pallas kernels  96.2 us (99%)
    pallas_call x1, Pallas kernels, on_device(): pl.pallas_call(kernel, out_shape=(shape((GRID, 8, 128), F32), shape((4096...  89.6 us
    pallas_call x1, Pallas kernels, on_device(): pl.pallas_call(last_kernel, out_shape=(shape((8192, 128), BF16), shape((C...  6.56 us

profile of v3, /device:TPU:1, one launch (start us, length us, event | category | flops | bytes accessed | tf_op | source)
XLA Modules:
  0.0 96.8 jit_solution(5003907334908045014)
XLA Ops:
  0.6 89.6 %shard_map.191 = (f32[64,8,128]{2,1,0:T(8,128)}, f32[4096,128]{1,0:T(8,128)}, bf16[4096,128]{1,0:T(8,128)(2,1)}, f32[32,64]{1,0:T(8,128)}, f32[2048,128]{1,0:T(8...) custom-call(bf16[8192,128]{1,0:T(8,128)(2,1)} %bitcast.35, bf16[4096,128]{1,0:T(8,128)(2,1)} %bitcast.36, ...), custom_call_target="tpu_custom_call" | custom-call | tf_op jit(solution)/shard_map/pallas_call | solution.py:675
  90.3 6.6 %shard_map.192 = (bf16[8192,128]{1,0:T(8,128)(2,1)}, f32[32,64]{1,0:T(8,128)}, f32[2048,128]{1,0:T(8,128)}, f32[2048,128]{1,0:T(8,128)}, f32[2048,128]{1,0:T(8,128)}) custom-call(f32[64,8,128]{2,1,0:T(8,128)} %get-tuple-element.17.last_hbm, f32[4096,128]{1,0:T(8,128)} %get-tuple-element.18.back_hbm, bf16[4096,128]{1,0:T(8,128)(2,1)} %get-tuple-element.19.half_hbm, ...), custom_call_target="tpu_custom_call" | custom-call | tf_op jit(solution)/shard_map/pallas_call | solution.py:722

commit v4 on v3

--- a/solution.py
+++ b/solution.py
@@ -159,7 +159,7 @@
                 )
         return 0
 
-    lax.fori_loop(0, 2, body, 0)
+    lax.fori_loop(0, 2, body, 0, unroll=2)
 
 
 TABLES = (
@@ -386,7 +386,7 @@
                     mixed[q, side * 2 + s, r * 8 : (r + 1) * 8, :] = sums[s][r]
             return 0
 
-        lax.fori_loop(0, 8, body, 0, unroll=2)
+        lax.fori_loop(0, 8, body, 0, unroll=4)
 
     need("spread")
     need_state(0, weight)
@@ -459,10 +459,10 @@
     total = lax.fori_loop(0, 32, local_grad, jnp.zeros((CO, C), F32), unroll=4)
     gx, gz, gy = lax.div(me, 16), lax.rem(lax.div(me, 4), 4), lax.rem(me, 4)
     rounds = (
+        (d, lambda j: {"dp": j}),
         (gy, lambda j: {"grid": me - gy + j}),
         (gz, lambda j: {"grid": me - 4 * gz + 4 * j}),
         (gx, lambda j: {"grid": me - 16 * gx + 16 * j}),
-        (d, lambda j: {"dp": j}),
     )
 
     def local_send(n, value):
@@ -540,7 +540,7 @@
             )
             return total + dot_exact(values, spread[q], NT)
 
-        total = lax.fori_loop(0, 8, body, jnp.zeros((64, 128), F32), unroll=2)
+        total = lax.fori_loop(0, 8, body, jnp.zeros((64, 128), F32), unroll=4)
         dsend[4 + t, pl.ds(side * 2, 2)] = total.reshape(2, 32, 128)
 
     wait_near(3)

time: 97 us -> 94.9 us (0.978)
  Pallas kernels: 96.2 us -> 94.1 us
    pallas_call x1, Pallas kernels: 89.6 us -> 87.7 us  [on_device(): pl.pallas_call(kernel, out_shape=(shape((GRID, 8, 128), F32), shape((4096...]
where the time goes in v4:
time: 94.9 us; the launch traced here: 94.7 us
  Pallas kernels  94.1 us (99%)
    pallas_call x1, Pallas kernels, on_device(): pl.pallas_call(kernel, out_shape=(shape((GRID, 8, 128), F32), shape((4096...  87.7 us
    pallas_call x1, Pallas kernels, on_device(): pl.pallas_call(last_kernel, out_shape=(shape((8192, 128), BF16), shape((C...  6.34 us

profile of v4, /device:TPU:1, one launch (start us, length us, event | category | flops | bytes accessed | tf_op | source)
XLA Modules:
  0.0 94.7 jit_solution(5420452218295892921)
XLA Ops:
  0.6 87.7 %shard_map.191 = (f32[64,8,128]{2,1,0:T(8,128)}, f32[4096,128]{1,0:T(8,128)}, bf16[4096,128]{1,0:T(8,128)(2,1)}, f32[32,64]{1,0:T(8,128)}, f32[2048,128]{1,0:T(8...) custom-call(bf16[8192,128]{1,0:T(8,128)(2,1)} %bitcast.35, bf16[4096,128]{1,0:T(8,128)(2,1)} %bitcast.36, ...), custom_call_target="tpu_custom_call" | custom-call | tf_op jit(solution)/shard_map/pallas_call | solution.py:675
  88.4 6.3 %shard_map.192 = (bf16[8192,128]{1,0:T(8,128)(2,1)}, f32[32,64]{1,0:T(8,128)}, f32[2048,128]{1,0:T(8,128)}, f32[2048,128]{1,0:T(8,128)}, f32[2048,128]{1,0:T(8,128)}) custom-call(f32[64,8,128]{2,1,0:T(8,128)} %get-tuple-element.17.last_hbm, f32[4096,128]{1,0:T(8,128)} %get-tuple-element.18.back_hbm, bf16[4096,128]{1,0:T(8,128)(2,1)} %get-tuple-element.19.half_hbm, ...), custom_call_target="tpu_custom_call" | custom-call | tf_op jit(solution)/shard_map/pallas_call | solution.py:722

commit v5 on v4

--- a/solution.py
+++ b/solution.py
@@ -150,7 +150,9 @@
                 for j in range(4) for s in range(2) for h in range(2)
             ]
             groups.append(jnp.concatenate(parts, axis=0).T)
-        result = dot_table(jnp.concatenate(groups, axis=0), table)
+        high, low = split(jnp.concatenate(groups, axis=0))
+        tables = jnp.concatenate([table[0], table[0], table[1]], axis=0)
+        result = dot(jnp.concatenate([high, low, high], axis=1), tables)
         for g in range(2):
             for j in range(4):
                 finish(
@@ -320,7 +322,9 @@
         dsend[m] = result.reshape(DP, 32, 128)
 
     def inverse_x(m, n):
-        result = table_dot(x_inv, drecv[m].reshape(128, 128))
+        high, low = split(drecv[m].reshape(128, 128))
+        tables = jnp.concatenate([x_inv[0], x_inv[0], x_inv[1]], axis=1)
+        result = dot(tables, jnp.concatenate([high, low, high], axis=0))
         gsend[n] = result.reshape(GRID, 8, 128)
 
     need("z_fwd")
@@ -363,10 +367,10 @@
         return pl.ds(((t * 4 + s) * 2 + c) * 16 + r * 8, 8)
 
     def mix(t, side):
-        high, low = split(drecv[t, pl.ds(side * 2, 2)].reshape(64, 128))
+        halves = jnp.concatenate(split(drecv[t, pl.ds(side * 2, 2)].reshape(64, 128)), axis=1)
 
         def body(q, _):
-            spectra = dot(high, spread[q]) + dot(low, spread[q])
+            spectra = dot(halves, jnp.concatenate([spread[q], spread[q]], axis=0))
             spec_x[q, pl.ds(pl.multiple_of(t * 128 + side * 64, 64), 64)] = spectra
             if t == 0:
                 sums = [[jnp.zeros((8, 128), F32) for _ in range(2)] for _ in range(2)]

time: 94.9 us -> 94.7 us (level)
  no operation moved by 1% of the time
where the time goes in v5:
time: 94.7 us; the launch traced here: 94.5 us
  Pallas kernels  93.8 us (99%)
    pallas_call x1, Pallas kernels, on_device(): pl.pallas_call(kernel, out_shape=(shape((GRID, 8, 128), F32), shape((4096...  87.6 us
    pallas_call x1, Pallas kernels, on_device(): pl.pallas_call(last_kernel, out_shape=(shape((8192, 128), BF16), shape((C...  6.2 us

profile of v5, /device:TPU:1, one launch (start us, length us, event | category | flops | bytes accessed | tf_op | source)
XLA Modules:
  0.0 94.5 jit_solution(29975540799958356)
XLA Ops:
  0.6 87.6 %shard_map.191 = (f32[64,8,128]{2,1,0:T(8,128)}, f32[4096,128]{1,0:T(8,128)}, bf16[4096,128]{1,0:T(8,128)(2,1)}, f32[32,64]{1,0:T(8,128)}, f32[2048,128]{1,0:T(8...) custom-call(bf16[8192,128]{1,0:T(8,128)(2,1)} %bitcast.35, bf16[4096,128]{1,0:T(8,128)(2,1)} %bitcast.36, ...), custom_call_target="tpu_custom_call" | custom-call | tf_op jit(solution)/shard_map/pallas_call | solution.py:679
  88.3 6.2 %shard_map.192 = (bf16[8192,128]{1,0:T(8,128)(2,1)}, f32[32,64]{1,0:T(8,128)}, f32[2048,128]{1,0:T(8,128)}, f32[2048,128]{1,0:T(8,128)}, f32[2048,128]{1,0:T(8,128)}) custom-call(f32[64,8,128]{2,1,0:T(8,128)} %get-tuple-element.17.last_hbm, f32[4096,128]{1,0:T(8,128)} %get-tuple-element.18.back_hbm, bf16[4096,128]{1,0:T(8,128)(2,1)} %get-tuple-element.19.half_hbm, ...), custom_call_target="tpu_custom_call" | custom-call | tf_op jit(solution)/shard_map/pallas_call | solution.py:726
